TPU v7x, 256 devices: a whole 4x4x8 slice. The times are simulated.
256 devices in a mesh: seq: 16 (over z_hi, y, core), res: 16 (over z_lo, x).
Axes of the slice: x: 4, y: 4, z: 8 (z_hi: 2, z_lo: 4; z = z_hi * 4 + z_lo), core: 2. Of those that a mesh axis runs over, the one named last changes fastest.
Arguments:
- alignment_embedding: bfloat16 [128, 2048, 256], P('seq', 'res'), may hold values from -6 to 6
- coupling_embedding: bfloat16 [2048, 2048, 128], P('res', 'seq'), may hold values from -6 to 6
- asking_projection: bfloat16 [256, 256], replicated, may hold values from -0.5 to 0.5
- lookup_projection: bfloat16 [256, 256], replicated, may hold values from -0.5 to 0.5
- content_projection: bfloat16 [256, 256], replicated, may hold values from -0.375 to 0.375
- filter_projection: bfloat16 [256, 256], replicated, may hold values from -0.375 to 0.375
- filter_offset: float32 [256], replicated, may hold values from -4 to 4
- coupling_head_projection: bfloat16 [128, 8], replicated, may hold values from -30 to 30, as said below
- final_projection: bfloat16 [256, 256], replicated, may hold values from -1.796875 to 1.796875
- final_offset: float32 [256], replicated, may hold values from -1.8 to 1.8
Outputs:
- update: bfloat16 [128, 2048, 256], P('seq', 'res')
Inputs may be any that keep to these rules, and one draw needn't show every extreme that they name: `coupling_head_projection`: a real matrix of head biases.
All inputs are finite; a program needn't handle non-finite values.
Results may differ from a plain program's by a relative error of at most 0.0065.
The roundings to bfloat16 on the way count: a program that leaves them out, or rounds other values in their place, can miss the bound.
Values may be sent and summed in bfloat16 or wider, within the bound.
A program may use at most 128 MiB of HBM per device.

v0:
```python
import jax
import jax.numpy as jnp
from jax import lax
from jax.sharding import PartitionSpec as P


def standardize_features(x):
    x = x.astype(jnp.float32)
    mean = jnp.mean(x, axis=-1, keepdims=True)
    var = jnp.mean((x - mean) ** 2, axis=-1, keepdims=True)
    return (x - mean) / jnp.sqrt(var + 1e-05)


def body(
    alignment_embedding,
    coupling_embedding,
    asking_projection,
    lookup_projection,
    content_projection,
    filter_projection,
    filter_offset,
    coupling_head_projection,
    final_projection,
    final_offset,
):
    alignment_strands, amino_shard, feature_depth = alignment_embedding.shape
    heads = coupling_head_projection.shape[1]
    head_size = feature_depth // heads
    scale = 1.0 / head_size**0.5
    pair_normed = standardize_features(coupling_embedding).astype(jnp.bfloat16)
    bias_tile = jnp.einsum(
        "ijc,ch->hij", pair_normed, coupling_head_projection, preferred_element_type=jnp.float32
    ).astype(jnp.bfloat16)
    bias_full = lax.all_gather(bias_tile, "seq", axis=2, tiled=True).astype(jnp.float32)
    standardized_embedding = standardize_features(alignment_embedding).astype(jnp.bfloat16)
    query = (
        jnp.dot(standardized_embedding, asking_projection, preferred_element_type=jnp.float32)
        * scale
    ).astype(jnp.bfloat16)
    sigmoid_filter = jax.nn.sigmoid(
        jnp.dot(standardized_embedding, filter_projection, preferred_element_type=jnp.float32)
        + filter_offset
    )
    key_local = jnp.dot(
        standardized_embedding, lookup_projection, preferred_element_type=jnp.float32
    ).astype(jnp.bfloat16)
    value_local = jnp.dot(
        standardized_embedding, content_projection, preferred_element_type=jnp.float32
    ).astype(jnp.bfloat16)
    key_all, value_all = (
        lax.all_gather(key_local, "res", axis=1, tiled=True),
        lax.all_gather(value_local, "res", axis=1, tiled=True),
    )
    total_res = key_all.shape[1]

    def lone_strand(items):
        q_row, k_row, v_row = items
        qh = q_row.reshape(amino_shard, heads, head_size)
        kh = k_row.reshape(total_res, heads, head_size)
        vh = v_row.reshape(total_res, heads, head_size)
        scores = jnp.einsum("qhd,khd->hqk", qh, kh, preferred_element_type=jnp.float32) + bias_full
        top = jnp.max(scores, axis=-1, keepdims=True)
        weights = jnp.exp(scores - top)
        total = jnp.sum(weights, axis=-1)
        mixed_features = jnp.einsum(
            "hqk,khd->qhd", weights.astype(jnp.bfloat16), vh, preferred_element_type=jnp.float32
        )
        return (mixed_features / jnp.transpose(total)[:, :, None]).reshape(
            amino_shard, feature_depth
        )

    mixed_features = lax.map(lone_strand, (query, key_all, value_all))
    filtered_update = (sigmoid_filter * mixed_features).astype(jnp.bfloat16)
    return (
        jnp.dot(filtered_update, final_projection, preferred_element_type=jnp.float32)
        + final_offset
    ).astype(jnp.bfloat16)


def solution(mesh):
    placed = (P("seq", "res", None), P("res", "seq", None), P(), P(), P(), P(), P(), P(), P(), P())
    return jax.shard_map(
        body, mesh=mesh, in_specs=placed, out_specs=P("seq", "res", None), check_vma=False
    )
```

profile of v0, /device:TPU:6, one launch (start us, length us, event | category | flops | bytes accessed | tf_op | source)
XLA Modules:
  0.0 439.3 jit_solution(10402077663725907175)
XLA Ops:
  6.5 0.0 copy-start
  6.5 0.0 all-gather.8.cloned.1.call-start
  6.5 3.5 convert_reduce_fusion
  10.1 6.0 %fusion.13 = f32[128,128]{1,0:T(8,128)S(1)} fusion(bf16[128,128,128]{2,1,0:T(8,128)(2,1)} %param.13, f32[128,128]{1,0:T(8,128)S(1)} %broadcast_multiply_fusion), kind=kLoop, calls=%fused_computation.16 | loop fusion | flops 8372224 | bytes 4325376 | tf_op jit(solution)/shard_map/reduce_sum | solution.py:10
  16.1 0.0 copy-done.7
  16.1 0.0 copy-done.1
  16.1 0.0 copy-start.2
  16.1 0.0 copy-start.3
  16.1 5.8 %fusion.15 = bf16[128,128,8]{1,2,0:T(8,128)(2,1)S(1)} fusion(bf16[128,128,128]{2,1,0:T(8,128)(2,1)S(1)} %copy-done.1, f32[128,128]{1,0:T(8,128)S(1)} %add_sqrt_fusion, f32[128,128]{1,0:T(8,128)S(1)} %broadcast_multiply_fusion, bf16[128,8]{0,1:T(8,128)(2,1)S(1)} %copy-done.7), kind=kOutput, calls=%fused_computation.18 | convolution fusion | flops 41943040 | bytes 4589568 | tf_op jit(solution)/shard_map/ijc,ch->hij/dot_general | solution.py:31
  22.0 0.7 copy.17
  22.7 0.0 all-gather.8.cloned.1.call-update
  22.8 0.0 all-gather.4.cloned.1.call-start
  22.8 0.0 copy-done.2
  22.8 0.2 convert_reduce_fusion.1
  23.0 0.4 fusion.27
  23.4 0.0 copy-done
  23.4 1.4 convolution_convert_fusion.1
  24.9 0.0 all-gather.4.cloned.1.call-update
  24.9 0.0 all-gather.6.cloned.1.call-start
  25.0 0.0 copy-done.3
  25.0 1.4 convolution_convert_fusion
  26.4 0.0 all-gather.6.cloned.1.call-update
  26.4 0.0 copy-done.4
  26.4 0.6 fusion.23
  27.1 76.9 %all-gather.8.cloned.1.call-done = bf16[8,128,2048]{2,1,0:T(8,128)(2,1)} async-done(((bf16[8,128,128]{2,1,0:T(8,128)(2,1)}), bf16[8,128,2048]{2,1,0:T(8,128)(2,1)}) %all-gather.8.cloned.1.call-update) | async-done | bytes 4194320 | tf_op jit(solution)/shard_map/all_gather | solution.py:34
  104.0 6.5 %convert_element_type.48 = f32[8,128,2048]{2,1,0:T(8,128)} convert(bf16[8,128,2048]{2,1,0:T(8,128)(2,1)} %all-gather.8.cloned.1.call-done) | non-fusion elementwise | flops 2097152 | bytes 12582912 | tf_op jit(solution)/shard_map/convert_element_type | solution.py:34
  110.5 116.9 %all-gather.4.cloned.1.call-done = bf16[8,2048,256]{1,2,0:T(8,128)(2,1)} async-done(((bf16[8,128,256]{1,2,0:T(8,128)(2,1)}), bf16[8,2048,256]{1,2,0:T(8,128)(2,1)}) %all-gather.4.cloned.1.call-update) | async-done | bytes 8388624 | tf_op jit(solution)/shard_map/all_gather | solution.py:52
  227.4 127.5 %all-gather.6.cloned.1.call-done = bf16[8,2048,256]{1,2,0:T(8,128)(2,1)} async-done(((bf16[8,128,256]{1,2,0:T(8,128)(2,1)}), bf16[8,2048,256]{1,2,0:T(8,128)(2,1)}) %all-gather.6.cloned.1.call-update) | async-done | bytes 8388624 | tf_op jit(solution)/shard_map/all_gather | solution.py:51
  354.9 76.0 %while.10 = (s32[]{:T(128)}, f32[8,128,256]{1,2,0:T(8,128)S(1)}, bf16[8,2048,256]{1,2,0:T(8,128)(2,1)}, bf16[8,128,256]{1,2,0:T(8,128)(2,1)S(1)}, bf16[8,2048,25...) while((s32[]{:T(128)}, f32[8,128,256]{1,2,0:T(8,128)S(1)}, bf16[8,2048,256]{1,2,0:T(8,128)(2,1)}, ...), condition=%wide.region_7.8_spmd, body=%wide.region_4.7_spmd.sunk | while | flops 281049088 | bytes 40456280 | solution.py:72
  354.9 1.8 constant_dynamic-slice_fusion.5
  356.8 4.8 %fusion.60 = (f32[8,128]{1,0:T(8,128)S(1)}, f32[8,128,2048]{2,1,0:T(8,128)S(1)}) fusion(f32[8,128,2048]{2,1,0:T(8,128)} %get-tuple-element.118, bf16[128,8,32]{0,2,1:T(8,128)(2,1)S(1)} %bitcast.55, bf16[2048,8,32]{0,2,1:T(8,128)(2,1)S(1)} %bitcast.52), kind=kOutput, calls=%fused_computation.53.clone.1 | convolution fusion | flops 138411008 | bytes 17895424 | tf_op jit(solution)/shard_map/while/body/eval_jaxpr/qhd,khd->hqk/dot_general | solution.py:61
  361.5 1.3 fusion.61
  362.8 1.6 fusion.62
  364.5 1.8 constant_dynamic-slice_fusion.5
  366.3 4.8 %fusion.60 = (f32[8,128]{1,0:T(8,128)S(1)}, f32[8,128,2048]{2,1,0:T(8,128)S(1)}) fusion(f32[8,128,2048]{2,1,0:T(8,128)} %get-tuple-element.118, bf16[128,8,32]{0,2,1:T(8,128)(2,1)S(1)} %bitcast.55, bf16[2048,8,32]{0,2,1:T(8,128)(2,1)S(1)} %bitcast.52), kind=kOutput, calls=%fused_computation.53.clone.1 | convolution fusion | flops 138411008 | bytes 17895424 | tf_op jit(solution)/shard_map/while/body/eval_jaxpr/qhd,khd->hqk/dot_general | solution.py:61
  371.0 1.3 fusion.61
  372.3 1.6 fusion.62
  374.0 1.8 constant_dynamic-slice_fusion.5
  375.8 4.8 %fusion.60 = (f32[8,128]{1,0:T(8,128)S(1)}, f32[8,128,2048]{2,1,0:T(8,128)S(1)}) fusion(f32[8,128,2048]{2,1,0:T(8,128)} %get-tuple-element.118, bf16[128,8,32]{0,2,1:T(8,128)(2,1)S(1)} %bitcast.55, bf16[2048,8,32]{0,2,1:T(8,128)(2,1)S(1)} %bitcast.52), kind=kOutput, calls=%fused_computation.53.clone.1 | convolution fusion | flops 138411008 | bytes 17895424 | tf_op jit(solution)/shard_map/while/body/eval_jaxpr/qhd,khd->hqk/dot_general | solution.py:61
  380.5 1.3 fusion.61
  381.8 1.6 fusion.62
  383.5 1.8 constant_dynamic-slice_fusion.5
  385.3 4.8 %fusion.60 = (f32[8,128]{1,0:T(8,128)S(1)}, f32[8,128,2048]{2,1,0:T(8,128)S(1)}) fusion(f32[8,128,2048]{2,1,0:T(8,128)} %get-tuple-element.118, bf16[128,8,32]{0,2,1:T(8,128)(2,1)S(1)} %bitcast.55, bf16[2048,8,32]{0,2,1:T(8,128)(2,1)S(1)} %bitcast.52), kind=kOutput, calls=%fused_computation.53.clone.1 | convolution fusion | flops 138411008 | bytes 17895424 | tf_op jit(solution)/shard_map/while/body/eval_jaxpr/qhd,khd->hqk/dot_general | solution.py:61
  390.0 1.3 fusion.61
  391.3 1.6 fusion.62
  393.0 1.8 constant_dynamic-slice_fusion.5
  394.8 4.8 %fusion.60 = (f32[8,128]{1,0:T(8,128)S(1)}, f32[8,128,2048]{2,1,0:T(8,128)S(1)}) fusion(f32[8,128,2048]{2,1,0:T(8,128)} %get-tuple-element.118, bf16[128,8,32]{0,2,1:T(8,128)(2,1)S(1)} %bitcast.55, bf16[2048,8,32]{0,2,1:T(8,128)(2,1)S(1)} %bitcast.52), kind=kOutput, calls=%fused_computation.53.clone.1 | convolution fusion | flops 138411008 | bytes 17895424 | tf_op jit(solution)/shard_map/while/body/eval_jaxpr/qhd,khd->hqk/dot_general | solution.py:61
  399.5 1.3 fusion.61
  400.8 1.6 fusion.62
  402.5 1.8 constant_dynamic-slice_fusion.5
  404.3 4.8 %fusion.60 = (f32[8,128]{1,0:T(8,128)S(1)}, f32[8,128,2048]{2,1,0:T(8,128)S(1)}) fusion(f32[8,128,2048]{2,1,0:T(8,128)} %get-tuple-element.118, bf16[128,8,32]{0,2,1:T(8,128)(2,1)S(1)} %bitcast.55, bf16[2048,8,32]{0,2,1:T(8,128)(2,1)S(1)} %bitcast.52), kind=kOutput, calls=%fused_computation.53.clone.1 | convolution fusion | flops 138411008 | bytes 17895424 | tf_op jit(solution)/shard_map/while/body/eval_jaxpr/qhd,khd->hqk/dot_general | solution.py:61
  409.0 1.3 fusion.61
  410.3 1.6 fusion.62
  412.0 1.8 constant_dynamic-slice_fusion.5
  413.8 4.8 %fusion.60 = (f32[8,128]{1,0:T(8,128)S(1)}, f32[8,128,2048]{2,1,0:T(8,128)S(1)}) fusion(f32[8,128,2048]{2,1,0:T(8,128)} %get-tuple-element.118, bf16[128,8,32]{0,2,1:T(8,128)(2,1)S(1)} %bitcast.55, bf16[2048,8,32]{0,2,1:T(8,128)(2,1)S(1)} %bitcast.52), kind=kOutput, calls=%fused_computation.53.clone.1 | convolution fusion | flops 138411008 | bytes 17895424 | tf_op jit(solution)/shard_map/while/body/eval_jaxpr/qhd,khd->hqk/dot_general | solution.py:61
  418.5 1.3 fusion.61
  419.8 1.6 fusion.62
  421.5 1.8 constant_dynamic-slice_fusion.5
  423.3 4.8 %fusion.60 = (f32[8,128]{1,0:T(8,128)S(1)}, f32[8,128,2048]{2,1,0:T(8,128)S(1)}) fusion(f32[8,128,2048]{2,1,0:T(8,128)} %get-tuple-element.118, bf16[128,8,32]{0,2,1:T(8,128)(2,1)S(1)} %bitcast.55, bf16[2048,8,32]{0,2,1:T(8,128)(2,1)S(1)} %bitcast.52), kind=kOutput, calls=%fused_computation.53.clone.1 | convolution fusion | flops 138411008 | bytes 17895424 | tf_op jit(solution)/shard_map/while/body/eval_jaxpr/qhd,khd->hqk/dot_general | solution.py:61
  428.0 1.3 fusion.61
  429.3 1.6 fusion.62
  431.0 0.0 copy-done.5
  431.0 0.0 copy-done.6
  431.0 1.8 fusion.24
  (30 shorter events, 0.3 us)
Async XLA Ops:
  6.5 16.9 %copy-start = (bf16[256,256]{1,0:T(8,128)(2,1)S(1)}, bf16[256,256]{1,0:T(8,128)(2,1)}, u32[]{:S(2)}) copy-start(bf16[256,256]{1,0:T(8,128)(2,1)} %param.16) | copy-start | bytes 393220
  6.5 9.6 %copy-start.7 = (bf16[128,8]{0,1:T(8,128)(2,1)S(1)}, bf16[128,8]{0,1:T(8,128)(2,1)}, u32[]{:S(2)}) copy-start(bf16[128,8]{0,1:T(8,128)(2,1)} %param.19) | copy-start | bytes 6148
  6.5 97.5 %all-gather.8.cloned.1.call-start = ((), (), s32[]{:S(2)}) async-start(), calls=%async_computation.2 | async-start | bytes 4456448 | tf_op jit(solution)/shard_map/all_gather | solution.py:34
  6.5 9.6 %copy-start.1 = (bf16[128,128,128]{2,1,0:T(8,128)(2,1)S(1)}, bf16[128,128,128]{2,1,0:T(8,128)(2,1)}, u32[]{:S(2)}) copy-start(bf16[128,128,128]{2,1,0:T(8,128)(2,1)} %param.13) | copy-start | bytes 12582916
  16.1 6.7 %copy-start.2 = (bf16[8,128,256]{2,1,0:T(8,128)(2,1)S(1)}, bf16[8,128,256]{2,1,0:T(8,128)(2,1)}, u32[]{:S(2)}) copy-start(bf16[8,128,256]{2,1,0:T(8,128)(2,1)} %param.12) | copy-start | bytes 1572868
  16.1 8.8 %copy-start.3 = (bf16[256,256]{1,0:T(8,128)(2,1)S(1)}, bf16[256,256]{1,0:T(8,128)(2,1)}, u32[]{:S(2)}) copy-start(bf16[256,256]{1,0:T(8,128)(2,1)} %param.15) | copy-start | bytes 393220
  22.0 4.5 %copy-start.4 = (bf16[256,256]{1,0:T(8,128)(2,1)S(1)}, bf16[256,256]{1,0:T(8,128)(2,1)}, u32[]{:S(2)}) copy-start(bf16[256,256]{1,0:T(8,128)(2,1)} %param.14) | copy-start | bytes 393220
  22.8 204.7 %all-gather.4.cloned.1.call-start = ((), (), s32[]{:S(2)}) async-start(), calls=%async_computation | async-start | bytes 8912896 | tf_op jit(solution)/shard_map/all_gather | solution.py:52
  24.9 330.0 %all-gather.6.cloned.1.call-start = ((), (), s32[]{:S(2)}) async-start(), calls=%async_computation.1 | async-start | bytes 8912896 | tf_op jit(solution)/shard_map/all_gather | solution.py:51
  354.9 76.0 %copy-start.5 = (bf16[256,256]{1,0:T(8,128)(2,1)S(1)}, bf16[256,256]{1,0:T(8,128)(2,1)}, u32[]{:S(2)}) copy-start(bf16[256,256]{1,0:T(8,128)(2,1)} %param.20) | copy-start | bytes 393220
  354.9 76.1 %copy-start.6 = (bf16[256,256]{1,0:T(8,128)(2,1)S(1)}, bf16[256,256]{1,0:T(8,128)(2,1)}, u32[]{:S(2)}) copy-start(bf16[256,256]{1,0:T(8,128)(2,1)} %param.17) | copy-start | bytes 393220
  354.9 76.1 %copy-start.8 = (f32[256]{0:T(256)S(1)}, f32[256]{0:T(256)}, u32[]{:S(2)}) copy-start(f32[256]{0:T(256)} %param.21) | copy-start | bytes 3076
  354.9 76.1 %copy-start.9 = (f32[256]{0:T(256)S(1)}, f32[256]{0:T(256)}, u32[]{:S(2)}) copy-start(f32[256]{0:T(256)} %param.18) | copy-start | bytes 3076
Sparse Core Ops, SparseCore 0:
  22.9 81.1 all-gather.7
  105.8 121.6 all-gather.3
  229.1 125.7 all-gather.5
where the time goes:
time: 441 us; the launch traced here: 439 us
  waiting for transfers between devices  321 us (73%)
  matrix products  62.1 us (14%)
  other arithmetic  26.7 us (6%)
  local copies, waits for them, and re-layouts  15.3 us (3%)
  between operations  13.3 us (3%)
    all_gather x1, waiting for transfers between devices, body(): lax.all_gather(key_local, 'res', axis=1, tiled=True)  127 us
    all_gather x1, waiting for transfers between devices, body(): lax.all_gather(value_local, 'res', axis=1, tiled=True)  117 us
    all_gather x1, waiting for transfers between devices, body(): lax.all_gather(bias_tile, 'seq', axis=2, tiled=True).astype(jnp.float32)  76.9 us
    dot_general x8, matrix products, lone_strand(): jnp.einsum('qhd,khd->hqk', qh, kh, preferred_element_type=jnp.float32)  38 us
    dynamic_slice x16, local copies, waits for them, and re-layouts, body(): mixed_features = lax.map(lone_strand, (query, key_all, value_all))  14.4 us
    dot_general x8, matrix products, lone_strand(): jnp.einsum('hqk,khd->qhd', weights.astype(jnp.bfloat16), vh, preferred_el...  13 us
    reduce_sum x8, other arithmetic, lone_strand(): total = jnp.sum(weights, axis=-1)  10.1 us
  transfers between devices with their start and end apart: 3, of which 3 were waited for; matrix products, arithmetic and copies ran while one was open for 2% of the time, Pallas kernels for 0%

commit v1 on v0

v1 whole, which is shorter than its diff:
```python
import functools
import math

import jax
import jax.numpy as jnp
from jax import lax
from jax.experimental import pallas as pl
from jax.experimental.pallas import tpu as pltpu
from jax.sharding import PartitionSpec as P

MESH = pl.DeviceIdType.MESH
VMEM_LIMIT = 60 * 1024 * 1024
HEAD_GROUPS = 4


def standardize_features(x):
    x = x.astype(jnp.float32)
    mean = jnp.mean(x, axis=-1, keepdims=True)
    var = jnp.mean((x - mean) ** 2, axis=-1, keepdims=True)
    return (x - mean) * lax.rsqrt(var + 1e-05)


def bias_tile_kernel(pair_ref, w_ref, out_ref, scratch):
    step = pl.program_id(0)
    block = pair_ref.shape[0]
    queries = out_ref.shape[2]
    heads = w_ref.shape[0]
    normed = standardize_features(pair_ref[...]).astype(jnp.bfloat16)
    w = w_ref[...]
    for i in range(block):
        tile = lax.dot_general(w, normed[i], (((1,), (1,)), ((), ())), preferred_element_type=jnp.float32)
        scratch[pl.ds(pl.multiple_of((step * block + i) * heads, heads), heads), :] = tile

    @pl.when(step == pl.num_programs(0) - 1)
    def _():
        for h in range(heads):
            tile = scratch[pl.ds(h, queries, stride=heads), :]
            out_ref[h] = tile.T.astype(jnp.bfloat16)


def bias_tile(pair, w_t):
    queries, keys, depth = pair.shape
    heads = w_t.shape[0]
    block = 16
    return pl.pallas_call(
        bias_tile_kernel,
        grid=(queries // block,),
        out_shape=jax.ShapeDtypeStruct((heads, keys, queries), jnp.bfloat16),
        in_specs=[
            pl.BlockSpec((block, keys, depth), lambda i: (i, 0, 0)),
            pl.BlockSpec((heads, depth), lambda i: (0, 0)),
        ],
        out_specs=pl.BlockSpec((heads, keys, queries), lambda i: (0, 0, 0)),
        scratch_shapes=[pltpu.VMEM((queries * heads, keys), jnp.float32)],
        compiler_params=pltpu.CompilerParams(vmem_limit_bytes=VMEM_LIMIT),
    )(pair, w_t)


def coordinates():
    s, r = lax.axis_index("seq"), lax.axis_index("res")
    return s % 2, (s // 2) % 4, s // 8, r % 4, r // 4


def exchange_kernel(
    n_ref, t_ref, nall_ref, ball_ref, lsem, zs, zr, xs, xr, bs, br, ys, yr, cs, cr
):
    c, y, zh, x, zl = coordinates()
    qh = zl // 2
    half = n_ref.shape[0] // 2
    groups = bs.shape[1]
    per = t_ref.shape[0] // groups

    def device(c_=c, y_=y, zh_=zh, x_=x, zl_=zl):
        return (zh_ * 8 + y_ * 2 + c_, zl_ * 4 + x_)

    z_peers = [device(zl_=(zl + d) % 4) for d in (1, 2, 3)]
    x_peers = [device(x_=(x + d) % 4) for d in (1, 2, 3)]
    y_peers = [device(y_=(y + d) % 4) for d in (1, 2, 3)]
    b_peers = [
        device(zl_=(zl + 2) % 4),
        device(zh_=1 - zh),
        device(zh_=1 - zh, zl_=(zl + 2) % 4),
    ]
    sibling = device(c_=1 - c)
    peers = z_peers + x_peers + y_peers + b_peers[1:] + [sibling]

    own_n = pltpu.make_async_copy(n_ref.at[pl.ds(qh * half, half)], nall_ref.at[:, x, zl], lsem.at[0])
    own_b = pltpu.make_async_copy(t_ref, ball_ref.at[:, c, y, zh, qh], lsem.at[1])
    own_n.start()
    own_b.start()

    barrier = pltpu.get_barrier_semaphore()
    for peer in peers:
        pl.semaphore_signal(barrier, inc=1, device_id=peer, device_id_type=MESH)
    pl.semaphore_wait(barrier, len(peers))

    def remote(src, dst, send, recv, peer):
        return pltpu.make_async_remote_copy(
            src_ref=src, dst_ref=dst, send_sem=send, recv_sem=recv, device_id=peer, device_id_type=MESH
        )

    def z_copy(k, d):
        to = (zl + d + 1) % 4
        return remote(
            n_ref.at[(to // 2) * half + k], nall_ref.at[k, x, zl], zs.at[k, d], zr.at[k, d], z_peers[d]
        )

    def x_copy(k, d):
        return remote(nall_ref.at[k, x], nall_ref.at[k, x], xs.at[k, d], xr.at[k, d], x_peers[d])

    def b_copy(g, d):
        at = pl.ds(g * per, per)
        return remote(
            t_ref.at[at], ball_ref.at[at, c, y, zh, qh], bs.at[d, g], br.at[d, g], b_peers[d]
        )

    def y_copy(g, d):
        at = pl.ds(g * per, per)
        return remote(ball_ref.at[at, c, y], ball_ref.at[at, c, y], ys.at[d, g], yr.at[d, g], y_peers[d])

    def c_copy(g):
        at = pl.ds(g * per, per)
        return remote(ball_ref.at[at, c], ball_ref.at[at, c], cs.at[g], cr.at[g], sibling)

    three = range(3)
    for k in range(max(half, groups)):
        if k < groups:
            for d in three:
                b_copy(k, d).start()
        if k < half:
            for d in three:
                z_copy(k, d).start()
    own_n.wait()
    own_b.wait()
    for k in range(max(half, groups)):
        if k < groups:
            for d in three:
                b_copy(k, d).wait_recv()
            for d in three:
                y_copy(k, d).start()
        if k < half:
            for d in three:
                z_copy(k, d).wait_recv()
            for d in three:
                x_copy(k, d).start()
    for g in range(groups):
        for d in three:
            y_copy(g, d).wait_recv()
        c_copy(g).start()
    for k in range(half):
        for d in three:
            x_copy(k, d).wait_recv()
    for g in range(groups):
        c_copy(g).wait_recv()
    for k in range(half):
        for d in three:
            z_copy(k, d).wait_send()
            x_copy(k, d).wait_send()
    for g in range(groups):
        for d in three:
            b_copy(g, d).wait_send()
            y_copy(g, d).wait_send()
        c_copy(g).wait_send()


def exchange(normed, tile):
    rows, block, depth = normed.shape
    heads = tile.shape[0]
    half = rows // 2
    sem = pltpu.SemaphoreType.DMA
    return pl.pallas_call(
        exchange_kernel,
        out_shape=(
            jax.ShapeDtypeStruct((half, 4, 4, block, depth), jnp.bfloat16),
            jax.ShapeDtypeStruct((heads, 2, 4, 2, 2, block, block), jnp.bfloat16),
        ),
        in_specs=[pl.BlockSpec(memory_space=pl.ANY)] * 2,
        out_specs=(pl.BlockSpec(memory_space=pl.ANY),) * 2,
        scratch_shapes=[
            sem((2,)),
            sem((half, 3)),
            sem((half, 3)),
            sem((half, 3)),
            sem((half, 3)),
            sem((3, HEAD_GROUPS)),
            sem((3, HEAD_GROUPS)),
            sem((3, HEAD_GROUPS)),
            sem((3, HEAD_GROUPS)),
            sem((HEAD_GROUPS,)),
            sem((HEAD_GROUPS,)),
        ],
        compiler_params=pltpu.CompilerParams(collective_id=0, has_side_effects=True),
    )(normed, tile)


NT = (((1,), (1,)), ((), ()))


def attention_kernel(
    n_ref, b_ref, wq_ref, wk_ref, wv_ref, wf_ref, off_ref, wo_ref, oo_ref,
    out_ref, k_scr, v_scr, q_scr, g_scr, a_scr, s_scr,
):
    h, r = pl.program_id(0), pl.program_id(1)
    heads = pl.num_programs(0)
    depth = wq_ref.shape[0]
    size = depth // 8
    keys = n_ref.shape[1]
    block = 128
    scale = 1.0 / size**0.5

    @pl.when(h == 0)
    def _():
        _, _, _, x, zl = coordinates()
        first = pl.multiple_of((x * 4 + zl % 2) * block, block)
        second = pl.multiple_of((x * 4 + zl % 2 + 2) * block, block)
        rows_q = jnp.concatenate([n_ref[r, pl.ds(first, block), :], n_ref[r, pl.ds(second, block), :]], axis=0)
        q = lax.dot_general(wq_ref[...], rows_q, NT, preferred_element_type=jnp.float32) * scale
        q_scr[r] = q.astype(jnp.bfloat16)
        gate = lax.dot_general(wf_ref[...], rows_q, NT, preferred_element_type=jnp.float32) + off_ref[...]
        g_scr[r] = jax.nn.sigmoid(gate)
        for at in range(0, keys, 512):
            part = n_ref[r, pl.ds(at, 512), :]
            k_scr[r, pl.ds(at, 512), :] = jnp.dot(part, wk_ref[...], preferred_element_type=jnp.float32).astype(jnp.bfloat16)
            v = lax.dot_general(wv_ref[...], part, NT, preferred_element_type=jnp.float32).astype(jnp.bfloat16)
            for hh in range(8):
                v_scr[r, hh, pl.ds(0, size), pl.ds(at, 512)] = v[hh * size:(hh + 1) * size]
                v_scr[r, hh, pl.ds(size, 16), pl.ds(at, 512)] = jnp.ones((16, 512), jnp.bfloat16)

    qt = q_scr[r]
    channel = lax.broadcasted_iota(jnp.int32, qt.shape, 0)
    qm = jnp.where(channel // size == h, qt, jnp.zeros_like(qt))
    top = None
    step = 256
    for at in range(0, keys, step):
        s = jnp.dot(k_scr[r, pl.ds(at, step), :], qm, preferred_element_type=jnp.float32)
        parts = []
        for sub in range(at // block, (at + step) // block):
            j = (sub % 4) * 4 + sub // 4
            at_j = (0, j % 2, (j // 2) % 4, j // 8)
            parts.append(jnp.concatenate([b_ref[at_j + (0,)], b_ref[at_j + (1,)]], axis=1))
        s = s + jnp.concatenate(parts, axis=0).astype(jnp.float32)
        s_scr[pl.ds(at, step), :] = s
        best = jnp.max(s, axis=0, keepdims=True)
        top = best if top is None else jnp.maximum(top, best)
    acc = None
    for at in range(0, keys, step):
        w = jnp.exp(s_scr[pl.ds(at, step), :] - top).astype(jnp.bfloat16)
        part = jnp.dot(v_scr[r, h, :, pl.ds(at, step)], w, preferred_element_type=jnp.float32)
        acc = part if acc is None else acc + part
    a_scr[r, pl.ds(pl.multiple_of(h * size, size), size), :] = acc[:size] / acc[size:size + 1]

    @pl.when(h == heads - 1)
    def _():
        gated = (g_scr[r] * a_scr[r]).T.astype(jnp.bfloat16)
        out = jnp.dot(gated, wo_ref[...], preferred_element_type=jnp.float32) + oo_ref[...]
        out_ref[r] = out.astype(jnp.bfloat16)


def attention(nall, ball, wq, wk, wv, wf, off, wo, oo):
    rows, _, _, block, depth = nall.shape
    keys = 16 * block
    heads = ball.shape[0]
    size = depth // heads
    whole = lambda a: pl.BlockSpec(a.shape, lambda h, r: (0,) * a.ndim)
    n = nall.reshape(rows, keys, depth)
    weights = (wq.T, wk, wv.T, wf.T, off.reshape(depth, 1), wo, oo.reshape(1, depth))
    return pl.pallas_call(
        attention_kernel,
        grid=(heads, rows),
        out_shape=jax.ShapeDtypeStruct((rows, 2 * block, depth), jnp.bfloat16),
        in_specs=[
            whole(n),
            pl.BlockSpec((1,) + ball.shape[1:], lambda h, r: (h, 0, 0, 0, 0, 0, 0)),
        ] + [whole(a) for a in weights],
        out_specs=pl.BlockSpec((rows, 2 * block, depth), lambda h, r: (0, 0, 0)),
        scratch_shapes=[
            pltpu.VMEM((rows, keys, depth), jnp.bfloat16),
            pltpu.VMEM((rows, heads, size + 16, keys), jnp.bfloat16),
            pltpu.VMEM((rows, depth, 2 * block), jnp.bfloat16),
            pltpu.VMEM((rows, depth, 2 * block), jnp.float32),
            pltpu.VMEM((rows, depth, 2 * block), jnp.float32),
            pltpu.VMEM((keys, 2 * block), jnp.float32),
        ],
        compiler_params=pltpu.CompilerParams(vmem_limit_bytes=VMEM_LIMIT),
    )(n, ball, *weights)


def body(
    alignment_embedding,
    coupling_embedding,
    asking_projection,
    lookup_projection,
    content_projection,
    filter_projection,
    filter_offset,
    coupling_head_projection,
    final_projection,
    final_offset,
):
    rows, block, depth = alignment_embedding.shape
    tile = bias_tile(coupling_embedding, coupling_head_projection.T)
    normed = standardize_features(alignment_embedding).astype(jnp.bfloat16)
    nall, ball = exchange(normed, tile)
    update = attention(
        nall, ball, asking_projection, lookup_projection, content_projection, filter_projection,
        filter_offset, final_projection, final_offset,
    )
    zl = lax.axis_index("res") // 4
    qh = zl // 2
    mine = lax.dynamic_slice_in_dim(update, qh * block, block, axis=1)
    theirs = lax.dynamic_slice_in_dim(update, (1 - qh) * block, block, axis=1)
    swap = [(r, (r + 8) % 16) for r in range(16)]
    other = lax.ppermute(theirs, "res", swap)
    first = jnp.where(qh == 0, mine, other)
    second = jnp.where(qh == 0, other, mine)
    return jnp.concatenate([first, second], axis=0)


def solution(mesh):
    placed = (P("seq", "res", None), P("res", "seq", None), P(), P(), P(), P(), P(), P(), P(), P())
    return jax.shard_map(
        body, mesh=mesh, in_specs=placed, out_specs=P("seq", "res", None), check_vma=False
    )
```

time: 441 us -> 158 us (0.36)
  waiting for transfers between devices: 321 us -> 13.7 us
  Pallas kernels: 0 us -> 127 us
  matrix products: 62.1 us -> 0 us
  other arithmetic: 26.7 us -> 6.73 us
  between operations: 13.3 us -> 0.06 us
  local copies, waits for them, and re-layouts: 15.3 us -> 7.4 us
    all_gather x3 -> x0, waiting for transfers between devices: 321 us -> none  [the longest x1 127 us: body(): lax.all_gather(key_local, 'res', axis=1, tiled=True)]
    pallas_call x0 -> x3, Pallas kernels: none -> 127 us  [the longest x1 72.7 us: exchange(): pl.pallas_call(exchange_kernel, out_shape=(jax.ShapeDtypeStruct((half, 4,...]
    dot_general x21 -> x0, matrix products: 62.1 us -> none  [the longest x8 38 us: lone_strand(): jnp.einsum('qhd,khd->hqk', qh, kh, preferred_element_type=jnp.float32)]
    ppermute x0 -> x1, waiting for transfers between devices: none -> 13.7 us  [body(): other = lax.ppermute(theirs, 'res', swap)]
    dynamic_slice x16 -> x1, local copies, waits for them, and re-layouts: 14.4 us -> 0.97 us  [body(): theirs = lax.dynamic_slice_in_dim(update, (1 - qh) * block, block, axis=1)]
    reduce_sum x8 -> x0, other arithmetic: 10.1 us -> none  [lone_strand(): total = jnp.sum(weights, axis=-1)]
    reduce_sum x2 -> x1, other arithmetic: 6.36 us -> 1.41 us  [standardize_features(): var = jnp.mean((x - mean) ** 2, axis=-1, keepdims=True)]
    unnamed x20 -> x3, local copies, waits for them, and re-layouts: 0.04 us -> 4.97 us
  transfers between devices with their start and end apart: 3 -> 1, of which waited for: 3 -> 1; matrix products, arithmetic and copies ran while one was open for 2% -> 0% of each run, Pallas kernels for 0% -> 0%
where the time goes in v1:
time: 158 us; the launch traced here: 155 us
  Pallas kernels  127 us (80%)
  waiting for transfers between devices  13.7 us (9%)
  local copies, waits for them, and re-layouts  7.4 us (5%)
  other arithmetic  6.73 us (4%)
    pallas_call x1, Pallas kernels, exchange(): pl.pallas_call(exchange_kernel, out_shape=(jax.ShapeDtypeStruct((half, 4,...  72.7 us
    pallas_call x1, Pallas kernels, attention(): pl.pallas_call(attention_kernel, grid=(heads, rows), out_shape=jax.ShapeD...  44.8 us
    ppermute x1, waiting for transfers between devices, body(): other = lax.ppermute(theirs, 'res', swap)  13.7 us
    pallas_call x1, Pallas kernels, bias_tile(): pl.pallas_call(bias_tile_kernel, grid=(queries // block,), out_shape=jax....  9.05 us
    unnamed x3, local copies, waits for them, and re-layouts  4.97 us
  transfers between devices with their start and end apart: 1, of which 1 were waited for; matrix products, arithmetic and copies ran while one was open for 0% of the time, Pallas kernels for 0%

profile of v1, /device:TPU:6, one launch (start us, length us, event | category | flops | bytes accessed | tf_op | source)
XLA Modules:
  0.0 155.0 jit_solution(6018726130548500308)
XLA Ops:
  0.0 1.2 convert_reduce_fusion
  1.3 1.4 fusion.2
  2.7 2.2 %fusion.3.n_ref = bf16[8,128,256]{2,1,0:T(8,128)(2,1)} fusion(bf16[8,128,256]{2,1,0:T(8,128)(2,1)} %param.10, f32[8,128]{1,0:T(8,128)S(1)} %add_rsqrt_fusion, f32[8,128]{1,0:T(8,128)S(1)} %broadcast_multiply_fusion), kind=kLoop, calls=%fused_computation.5 | loop fusion | flops 1048576 | bytes 1056768 | tf_op jit(solution)/shard_map/convert_element_type | solution.py:302
  4.9 1.6 %copy.14 = bf16[256,256]{0,1:T(8,128)(2,1)} copy(bf16[256,256]{1,0:T(8,128)(2,1)} %param.12) | data formatting | bytes 262144 | tf_op args[2]
  6.5 1.7 %copy.15 = bf16[256,256]{0,1:T(8,128)(2,1)} copy(bf16[256,256]{1,0:T(8,128)(2,1)} %param.14) | data formatting | bytes 262144 | tf_op args[4]
  8.2 1.7 %copy.16 = bf16[256,256]{0,1:T(8,128)(2,1)} copy(bf16[256,256]{1,0:T(8,128)(2,1)} %param.15) | data formatting | bytes 262144 | tf_op args[5]
  9.8 1.5 copy.17.off_ref
  11.3 9.0 %shard_map.100.t_ref = bf16[8,128,128]{2,1,0:T(8,128)(2,1)} custom-call(bf16[128,128,128]{2,1,0:T(8,128)(2,1)} %pair_ref.1, bf16[8,128]{1,0:T(8,128)(2,1)} %bitcast.11), custom_call_target="tpu_custom_call" | custom-call | tf_op jit(solution)/shard_map/pallas_call | solution.py:45
  20.4 72.7 %shard_map.101 = (bf16[4,4,4,128,256]{4,3,2,1,0:T(8,128)(2,1)}, bf16[8,2,4,2,2,128,128]{6,5,4,3,2,1,0:T(8,128)(2,1)}) custom-call(bf16[8,128,256]{2,1,0:T(8,128)(2,1)} %fusion.3.n_ref, bf16[8,128,128]{2,1,0:T(8,128)(2,1)} %shard_map.100.t_ref), custom_call_target="tpu_custom_call" | custom-call | tf_op jit(solution)/shard_map/pallas_call | solution.py:171
  93.1 44.8 %shard_map.102 = bf16[4,256,256]{2,1,0:T(8,128)(2,1)} custom-call(bf16[4,2048,256]{2,1,0:T(8,128)(2,1)} %bitcast.7, bf16[8,2,4,2,2,128,128]{6,5,4,3,2,1,0:T(8,128)(2,1)} %get-tuple-element.8.b_ref, bf16[256,256]{1,0:T(8,128)(2,1)} %bitcast.8, bf16[256,256]{1,0:T(8,128)(2,1)} %wk_ref.1, bf16[256,256]{1,0:T(8,128)(2,1)} %bitcast.9, bf16[256,256]{1,0:T(8,128)(2,1)} %bitcast.10, ...), custom_call_target="tpu_custom_call" | custom-call | tf_op jit(solution)/shard_map/pallas_call | solution.py:267
  137.9 1.0 constant_dynamic-slice_fusion
  138.9 0.5 collective-permute-start
  139.4 13.7 %collective-permute-done = bf16[4,128,256]{2,1,0:T(8,128)(2,1)S(1)} collective-permute-done((bf16[4,128,256]{2,1,0:T(8,128)(2,1)S(1)}, bf16[4,128,256]{2,1,0:T(8,128)(2,1)S(1)}, u32[]{:S(2)}, u32[]{:S(2)}) %collective-permute-start) | collective-permute-done | bytes 262176 | tf_op jit(solution)/shard_map/ppermute | solution.py:313
  153.1 1.0 broadcast_select_fusion.1
  154.1 0.8 pad_maximum_fusion
  (2 shorter events, 0.0 us)
Async XLA Ops:
  138.9 14.2 %collective-permute-start = (bf16[4,128,256]{2,1,0:T(8,128)(2,1)S(1)}, bf16[4,128,256]{2,1,0:T(8,128)(2,1)S(1)}, u32[]{:S(2)}, u32[]{:S(2)}) collective-permute-start(bf16[4,128,256]{2,1,0:T(8,128)(2,1)S(1)} %constant_dynamic-slice_fusion), channel_id=1, source_target_pairs={{0,8},{1,9},{2,10},{3,11},{4,12},{5,13},{6,14},{7,15},{8,0},{9,1},... | collective-permute-start | bytes 786440 | tf_op jit(solution)/shard_map/ppermute | solution.py:313

commit v2 on v0

v2 whole, which is shorter than its diff:
```python
import jax
import jax.numpy as jnp
from jax import lax
from jax.experimental import pallas as pl
from jax.experimental.pallas import tpu as pltpu
from jax.sharding import PartitionSpec as P

MESH = pl.DeviceIdType.MESH
VMEM_LIMIT = 62 * 1024 * 1024
NT = (((1,), (1,)), ((), ()))
HEADS = 8
HALF = 4
BLOCK = 128
STEP = 256
TILES = (
    [(0, 0), (1, 0)]
    + [(0, 1), (1, 1)]
    + [(0, 2), (1, 2), (2, 0), (2, 1), (2, 2)]
    + [(0, 3), (1, 3), (2, 3)]
    + [(0, 4), (1, 4), (2, 4), (3, 0), (3, 1)]
    + [(0, 5), (1, 5), (2, 5), (3, 2)]
    + [(0, 6), (1, 6), (2, 6), (3, 3), (3, 4), (3, 5)]
    + [(3, 6), (0, 7), (1, 7), (2, 7), (3, 7)]
)
DONE = (
    (0, 0, 0), (0, 0, 0), (1, 1, 2), (3, 4, 4), (5, 6, 9), (10, 12, 12), (13, 15, 17), (18, 20, 21), (22, 27, 27),
    (32, 32, 32),
)


def lookup(table, index):
    value = jnp.int32(table[0])
    for at in range(1, len(table)):
        if table[at] != table[at - 1]:
            value = value + jnp.where(index >= at, table[at] - table[at - 1], 0).astype(jnp.int32)
    return value


def standardize_features(x):
    x = x.astype(jnp.float32)
    mean = jnp.mean(x, axis=-1, keepdims=True)
    var = jnp.mean((x - mean) ** 2, axis=-1, keepdims=True)
    return (x - mean) * lax.rsqrt(var + 1e-05)


def fused_kernel(
    m_ref, pair_ref, wq_ref, wk_ref, wv_ref, wf_ref, off_ref, wc_ref, wo_ref, oo_ref,
    out_ref,
    nown, nall, tile, ball, pair_buf, raw, k_scr, v_scr, q_scr, g_scr, a_scr, s_scr, upd, wqt, wvt,
    psem, lsem, zs, zr, xs, xr, bs, br, ys, yr, cs, cr, os, orr,
):
    s, res = lax.axis_index("seq"), lax.axis_index("res")
    c, y, zh, x, zl = s % 2, (s // 2) % 4, s // 8, res % 4, res // 4
    qh = zl // 2
    depth = wq_ref.shape[0]
    size = depth // HEADS
    keys = k_scr.shape[1]
    scale = 1.0 / size**0.5

    def device(c_=c, y_=y, zh_=zh, x_=x, zl_=zl):
        return (zh_ * 8 + y_ * 2 + c_, zl_ * 4 + x_)

    z_peers = [device(zl_=(zl + d) % 4) for d in (1, 2, 3)]
    x_left, x_right = device(x_=(x + 3) % 4), device(x_=(x + 1) % 4)
    y_left, y_right = device(y_=(y + 3) % 4), device(y_=(y + 1) % 4)
    partner = device(zl_=(zl + 2) % 4)
    b_peers = [partner, device(zh_=1 - zh), device(zh_=1 - zh, zl_=(zl + 2) % 4)]
    sibling = device(c_=1 - c)
    peers = z_peers + [x_left, x_right, y_left, y_right] + b_peers[1:] + [sibling]

    barrier = pltpu.get_barrier_semaphore()
    for peer in peers:
        pl.semaphore_signal(barrier, inc=1, device_id=peer, device_id_type=MESH)

    chunk = BLOCK // 4

    def pair_copy(i):
        at = pl.ds(i * chunk, chunk)
        return pltpu.make_async_copy(pair_ref.at[at], pair_buf.at[at], psem.at[i])

    for i in range(4):
        pair_copy(i).start()

    def norm_row(i, carry):
        nown[i] = standardize_features(m_ref[i]).astype(jnp.bfloat16)
        return carry

    lax.fori_loop(0, 2 * HALF, norm_row, 0)

    def remote(src, dst, send, recv, peer):
        return pltpu.make_async_remote_copy(
            src_ref=src, dst_ref=dst, send_sem=send, recv_sem=recv, device_id=peer, device_id_type=MESH
        )

    def z_copy(k, d):
        to = (zl + d + 1) % 4
        return remote(nown.at[(to // 2) * HALF + k], nall.at[k, x, zl], zs.at[k, d], zr.at[k, d], z_peers[d])

    def x_copy(k, d):
        return remote(nall.at[k, x], nall.at[k, x], xs.at[k, d], xr.at[k, d], (x_right, x_left)[d])

    def x_forward(k, d):
        block = nall.at[k, (x + 3) % 4, pl.ds(0, 2)] if d == 0 else nall.at[k, (x + 1) % 4, pl.ds(2, 2)]
        return remote(block, block, xs.at[k, 2 + d], xr.at[k, 2 + d], (x_right, x_left)[d])

    def b_copy(h, d):
        return remote(tile.at[h], ball.at[h, c, y, zh, qh], bs.at[h, d], br.at[h, d], b_peers[d])

    def y_copy(h, d):
        return remote(ball.at[h, c, y], ball.at[h, c, y], ys.at[h, d], yr.at[h, d], (y_right, y_left)[d])

    def y_forward(h, d):
        block = ball.at[h, c, (y + 3) % 4, 0] if d == 0 else ball.at[h, c, (y + 1) % 4, 1]
        return remote(block, block, ys.at[h, 2 + d], yr.at[h, 2 + d], (y_right, y_left)[d])

    def c_copy(h):
        return remote(ball.at[h, c], ball.at[h, c], cs.at[h], cr.at[h], sibling)

    def out_copy(r):
        return remote(
            upd.at[r, pl.ds((1 - qh) * BLOCK, BLOCK)], out_ref.at[qh * HALF + r], os.at[r], orr.at[r], partner
        )

    own_n = pltpu.make_async_copy(nown.at[pl.ds(qh * HALF, HALF)], nall.at[:, x, zl], lsem.at[0])
    own_b = pltpu.make_async_copy(tile, ball.at[:, c, y, zh, qh], lsem.at[1])

    pl.semaphore_wait(barrier, len(peers))
    own_n.start()

    def start_z(k, carry):
        for d in range(3):
            z_copy(k, d).start()
        return carry

    lax.fori_loop(0, HALF, start_z, 0)

    wqt[...] = wq_ref[...].astype(jnp.float32).T.astype(jnp.bfloat16)
    wvt[...] = wv_ref[...].astype(jnp.float32).T.astype(jnp.bfloat16)
    for r in range(HALF):
        v_scr[r, :, pl.ds(size, 16), :] = jnp.ones((HEADS, 16, keys), jnp.bfloat16)

    wc = wc_ref[...]
    group = 8

    def pair_rows(i, carry):
        at = pl.multiple_of(i * group, group)
        normed = standardize_features(pair_buf[pl.ds(at, group)]).astype(jnp.bfloat16)
        for j in range(group):
            raw[pl.ds(pl.multiple_of((at + j) * HEADS, HEADS), HEADS), :] = lax.dot_general(
                wc, normed[j], NT, preferred_element_type=jnp.float32
            )
        return carry

    def wait_z(k):
        for d in range(3):
            z_copy(k, d).wait_recv()
        for d in range(2):
            x_copy(k, d).start()

    for i in range(4):
        pair_copy(i).wait()
        lax.fori_loop(i * (chunk // group), (i + 1) * (chunk // group), pair_rows, 0)
        if i == 2:
            own_n.wait()
            wait_z(0)
    for h in range(HEADS):
        tile[h] = raw[pl.ds(h, BLOCK, stride=HEADS), :].T.astype(jnp.bfloat16)
    own_b.start()

    def start_b(h, carry):
        for d in range(3):
            b_copy(h, d).start()
        return carry

    lax.fori_loop(0, HEADS, start_b, 0)
    own_b.wait()

    def project(r):
        first = zl % 2
        rows_q = jnp.concatenate([nall[r, x, first], nall[r, x, first + 2]], axis=0)
        q = lax.dot_general(wqt[...], rows_q, NT, preferred_element_type=jnp.float32) * scale
        q_scr[r] = q.astype(jnp.bfloat16)
        g_scr[r] = jax.nn.sigmoid(
            jnp.dot(rows_q, wf_ref[...], preferred_element_type=jnp.float32) + off_ref[...]
        )

        def part(i, carry):
            rows = nall[r, i].reshape(4 * BLOCK, depth)
            at = pl.multiple_of(i * 4 * BLOCK, 4 * BLOCK)
            k_scr[r, pl.ds(at, 4 * BLOCK), :] = jnp.dot(
                rows, wk_ref[...], preferred_element_type=jnp.float32
            ).astype(jnp.bfloat16)
            v = lax.dot_general(wvt[...], rows, NT, preferred_element_type=jnp.float32).astype(jnp.bfloat16)
            for h in range(HEADS):
                v_scr[r, h, pl.ds(0, size), pl.ds(at, 4 * BLOCK)] = v[h * size:(h + 1) * size]
            return carry

        lax.fori_loop(0, 4, part, 0)

    def attend(r, h):
        qt = q_scr[r]
        channel = lax.broadcasted_iota(jnp.int32, qt.shape, 0)
        qm = jnp.where((channel >= h * size) & (channel < (h + 1) * size), qt, jnp.zeros_like(qt))
        top = None
        for at in range(0, keys, STEP):
            scores = jnp.dot(k_scr[r, pl.ds(at, STEP), :], qm, preferred_element_type=jnp.float32)
            parts = []
            for sub in range(at // BLOCK, (at + STEP) // BLOCK):
                j = (sub % 4) * 4 + sub // 4
                here = (h, j % 2, (j // 2) % 4, j // 8)
                parts.append(jnp.concatenate([ball[here + (0,)], ball[here + (1,)]], axis=1))
            scores = scores + jnp.concatenate(parts, axis=0).astype(jnp.float32)
            s_scr[pl.ds(at, STEP), :] = scores
            best = jnp.max(scores, axis=0, keepdims=True)
            top = best if top is None else jnp.maximum(top, best)
        acc = None
        for at in range(0, keys, STEP):
            weights = jnp.exp(s_scr[pl.ds(at, STEP), :] - top).astype(jnp.bfloat16)
            part = jnp.dot(v_scr[r, h, :, pl.ds(at, STEP)], weights, preferred_element_type=jnp.float32)
            acc = part if acc is None else acc + part
        a_scr[r, pl.ds(pl.multiple_of(h * size, size), size), :] = acc[:size] / acc[size:size + 1]

    def finish(r):
        gated = (g_scr[r] * a_scr[r].T).astype(jnp.bfloat16)
        update = jnp.dot(gated, wo_ref[...], preferred_element_type=jnp.float32) + oo_ref[...]
        upd[r] = update.astype(jnp.bfloat16)
        out_copy(r).start()
        out_ref[qh * HALF + r] = upd[r, pl.ds(pl.multiple_of(qh * BLOCK, BLOCK), BLOCK), :]

    tile_rows, tile_heads = [t[0] for t in TILES], [t[1] for t in TILES]

    def run_tile(i, carry):
        r, h = lookup(tile_rows, i), lookup(tile_heads, i)
        attend(r, h)
        pl.when(h == HEADS - 1)(lambda: finish(r))
        return carry

    def run_tiles(first, last):
        lax.fori_loop(first, last, run_tile, 0)

    def tick(t, done):
        even = t % 2 == 0
        k = t // 2
        after = [lookup([d[p] for d in DONE], t) for p in range(3)]

        @pl.when(t < HEADS)
        def _():
            for d in range(3):
                b_copy(t, d).wait_recv()
            for d in range(2):
                y_copy(t, d).start()

        @pl.when(even & (k < HALF))
        def _():
            for d in range(2):
                x_copy(k, d).wait_recv()
            for d in range(2):
                x_forward(k, d).start()

        @pl.when(t >= 2)
        def _():
            c_copy(t - 2).wait_recv()

        run_tiles(done, after[0])

        @pl.when((t >= 1) & (t <= HEADS))
        def _():
            for d in range(2):
                y_forward(t - 1, d).wait_recv()
            c_copy(t - 1).start()

        @pl.when(even & (k < HALF - 1))
        def _():
            wait_z(k + 1)

        run_tiles(after[0], after[1])

        @pl.when(t < HEADS)
        def _():
            for d in range(2):
                y_copy(t, d).wait_recv()
            for d in range(2):
                y_forward(t, d).start()

        @pl.when(even & (k < HALF))
        def _():
            for d in range(2):
                x_forward(k, d).wait_recv()
            project(k)

        run_tiles(after[1], after[2])
        return after[2]

    lax.fori_loop(0, len(DONE), tick, jnp.int32(0))

    def close_rows(k, carry):
        out_copy(k).wait_recv()
        out_copy(k).wait_send()
        for d in range(3):
            z_copy(k, d).wait_send()
        for d in range(2):
            x_copy(k, d).wait_send()
            x_forward(k, d).wait_send()
        return carry

    def close_heads(h, carry):
        for d in range(3):
            b_copy(h, d).wait_send()
        for d in range(2):
            y_copy(h, d).wait_send()
            y_forward(h, d).wait_send()
        c_copy(h).wait_send()
        return carry

    lax.fori_loop(0, HEADS, close_heads, 0)
    lax.fori_loop(0, HALF, close_rows, 0)


def body(
    alignment_embedding,
    coupling_embedding,
    asking_projection,
    lookup_projection,
    content_projection,
    filter_projection,
    filter_offset,
    coupling_head_projection,
    final_projection,
    final_offset,
):
    rows, block, depth = alignment_embedding.shape
    heads = coupling_head_projection.shape[1]
    size = depth // heads
    keys = 16 * block
    bf, f32 = jnp.bfloat16, jnp.float32
    sem = pltpu.SemaphoreType.DMA
    vmem = pl.BlockSpec(memory_space=pltpu.VMEM)
    in_specs = [vmem] * 10
    in_specs[1] = pl.BlockSpec(memory_space=pl.ANY)
    return pl.pallas_call(
        fused_kernel,
        out_shape=jax.ShapeDtypeStruct((rows, block, depth), bf),
        in_specs=in_specs,
        out_specs=vmem,
        scratch_shapes=[
            pltpu.VMEM((rows, block, depth), bf),
            pltpu.VMEM((HALF, 4, 4, block, depth), bf),
            pltpu.VMEM((heads, block, block), bf),
            pltpu.VMEM((heads, 2, 4, 2, 2, block, block), bf),
            pltpu.VMEM((block, block, coupling_embedding.shape[2]), bf),
            pltpu.VMEM((block * heads, block), f32),
            pltpu.VMEM((HALF, keys, depth), bf),
            pltpu.VMEM((HALF, heads, size + 16, keys), bf),
            pltpu.VMEM((HALF, depth, 2 * block), bf),
            pltpu.VMEM((HALF, 2 * block, depth), f32),
            pltpu.VMEM((HALF, depth, 2 * block), f32),
            pltpu.VMEM((keys, 2 * block), f32),
            pltpu.VMEM((HALF, 2 * block, depth), bf),
            pltpu.VMEM((depth, depth), bf),
            pltpu.VMEM((depth, depth), bf),
            sem((4,)),
            sem((2,)),
            sem((HALF, 3)),
            sem((HALF, 3)),
            sem((HALF, 4)),
            sem((HALF, 4)),
            sem((heads, 3)),
            sem((heads, 3)),
            sem((heads, 4)),
            sem((heads, 4)),
            sem((heads,)),
            sem((heads,)),
            sem((HALF,)),
            sem((HALF,)),
        ],
        compiler_params=pltpu.CompilerParams(
            collective_id=0, has_side_effects=True, vmem_limit_bytes=VMEM_LIMIT
        ),
    )(
        alignment_embedding, coupling_embedding, asking_projection, lookup_projection, content_projection,
        filter_projection, filter_offset.reshape(1, depth), coupling_head_projection.T, final_projection,
        final_offset.reshape(1, depth),
    )


def solution(mesh):
    placed = (P("seq", "res", None), P("res", "seq", None), P(), P(), P(), P(), P(), P(), P(), P())
    return jax.shard_map(
        body, mesh=mesh, in_specs=placed, out_specs=P("seq", "res", None), check_vma=False
    )
```

time: 441 us -> 131 us (0.30)
  waiting for transfers between devices: 321 us -> 0 us
  Pallas kernels: 0 us -> 127 us
  matrix products: 62.1 us -> 0 us
  other arithmetic: 26.7 us -> 0 us
  local copies, waits for them, and re-layouts: 15.3 us -> 1.87 us
  between operations: 13.3 us -> 0.01 us
    all_gather x3 -> x0, waiting for transfers between devices: 321 us -> none  [the longest x1 127 us: body(): lax.all_gather(key_local, 'res', axis=1, tiled=True)]
    pallas_call x0 -> x1, Pallas kernels: none -> 127 us  [body(): pl.pallas_call(fused_kernel, out_shape=jax.ShapeDtypeStruct((rows, block,...]
    dot_general x21 -> x0, matrix products: 62.1 us -> none  [the longest x8 38 us: lone_strand(): jnp.einsum('qhd,khd->hqk', qh, kh, preferred_element_type=jnp.float32)]
    reduce_sum x12 -> x0, other arithmetic: 20.2 us -> none  [the longest x8 10.1 us: lone_strand(): total = jnp.sum(weights, axis=-1)]
    dynamic_slice x16 -> x0, local copies, waits for them, and re-layouts: 14.4 us -> none  [body(): mixed_features = lax.map(lone_strand, (query, key_all, value_all))]
    convert_element_type x1 -> x0, other arithmetic: 6.47 us -> none  [body(): lax.all_gather(bias_tile, 'seq', axis=2, tiled=True).astype(jnp.float32)]
  transfers between devices with their start and end apart: 3 -> 0, of which waited for: 3 -> 0; matrix products, arithmetic and copies ran while one was open for 2% -> 0% of each run, Pallas kernels for 0% -> 0%
where the time goes in v2:
time: 131 us; the launch traced here: 129 us
  Pallas kernels  127 us (97%)
  local copies, waits for them, and re-layouts  1.87 us (1%)
    pallas_call x1, Pallas kernels, body(): pl.pallas_call(fused_kernel, out_shape=jax.ShapeDtypeStruct((rows, block,...  127 us

profile of v2, /device:TPU:6, one launch (start us, length us, event | category | flops | bytes accessed | tf_op | source)
XLA Modules:
  0.0 128.9 jit_solution(13896137133536628886)
XLA Ops:
  0.0 127.0 %shard_map.100 = bf16[8,128,256]{2,1,0:T(8,128)(2,1)} custom-call(bf16[8,128,256]{2,1,0:T(8,128)(2,1)} %m_ref.1, bf16[128,128,128]{2,1,0:T(8,128)(2,1)} %pair_ref.1, bf16[256,256]{1,0:T(8,128)(2,1)} %wq_ref.1, bf16[256,256]{1,0:T(8,128)(2,1)} %wk_ref.1, bf16[256,256]{1,0:T(8,128)(2,1)} %wv_ref.1, bf16[256,256]{1,0:T(8,128)(2,1)} %wf_ref.1, ...), custom_call_target="tpu_custom_call" | custom-call | tf_op jit(solution)/shard_map/pallas_call | solution.py:340
  127.0 1.9 %copy.12 = bf16[8,128,256]{2,1,0:T(8,128)(2,1)} copy(bf16[8,128,256]{2,1,0:T(8,128)(2,1)} %shard_map.100) | data formatting | bytes 1048576

commit v3 on v2

--- a/solution.py
+++ b/solution.py
@@ -12,27 +12,32 @@
 HALF = 4
 BLOCK = 128
 STEP = 256
+STEPS = (
+    0, 1, 3, 3, 4, 1, 3, 4, 2, 5, 2, 0, 6, 4, 7, 7, 5, 3, 5, 6, 7, 3, 7, 6, 7,
+    4, 7, 1, 0, 4, 5, 3, 2, 6, 5, 7, 3, 7, 7, 6, 4, 7, 3, 1, 7, 7, 4, 7, 7, 5,
+    7, 2, 4, 6, 7, 5, 7, 7, 7, 6, 5, 7, 7, 7, 6, 7, 7, 7, 7, 7, 7, 7, 7, 7, 7,
+)
 TILES = (
-    [(0, 0), (1, 0)]
-    + [(0, 1), (1, 1)]
-    + [(0, 2), (1, 2), (2, 0), (2, 1), (2, 2)]
-    + [(0, 3), (1, 3), (2, 3)]
-    + [(0, 4), (1, 4), (2, 4), (3, 0), (3, 1)]
-    + [(0, 5), (1, 5), (2, 5), (3, 2)]
-    + [(0, 6), (1, 6), (2, 6), (3, 3), (3, 4), (3, 5)]
-    + [(3, 6), (0, 7), (1, 7), (2, 7), (3, 7)]
+    0, 8, 1, 9, 2, 10, 16, 17, 18, 3, 11, 19, 4, 12, 20, 24,
+    25, 26, 27, 28, 5, 13, 21, 29, 6, 14, 22, 30, 7, 15, 23, 31,
 )
-DONE = (
-    (0, 0, 0), (0, 0, 0), (1, 1, 2), (3, 4, 4), (5, 6, 9), (10, 12, 12), (13, 15, 17), (18, 20, 21), (22, 27, 27),
-    (32, 32, 32),
-)
+
+
+def packed(values, bits):
+    per = 30 // bits
+    return per, [sum(v << (bits * at) for at, v in enumerate(values[i:i + per])) for i in range(0, len(values), per)]
+
+
+def unpacked(values, bits, index):
+    per, words = packed(values, bits)
+    word = lookup(words, index // per)
+    return (word >> (bits * (index % per))) % (1 << bits)
 
 
 def lookup(table, index):
     value = jnp.int32(table[0])
     for at in range(1, len(table)):
-        if table[at] != table[at - 1]:
-            value = value + jnp.where(index >= at, table[at] - table[at - 1], 0).astype(jnp.int32)
+        value = jnp.where(index >= at, jnp.int32(table[at]), value)
     return value
 
 
@@ -46,7 +51,7 @@
 def fused_kernel(
     m_ref, pair_ref, wq_ref, wk_ref, wv_ref, wf_ref, off_ref, wc_ref, wo_ref, oo_ref,
     out_ref,
-    nown, nall, tile, ball, pair_buf, raw, k_scr, v_scr, q_scr, g_scr, a_scr, s_scr, upd, wqt, wvt,
+    nown, nall, tile, ball, pair_buf, raw, k_scr, v_scr, q_scr, g_scr, a_scr, s_even, s_odd, t_even, t_odd, upd, wqt, wvt,
     psem, lsem, zs, zr, xs, xr, bs, br, ys, yr, cs, cr, os, orr,
 ):
     s, res = lax.axis_index("seq"), lax.axis_index("res")
@@ -127,12 +132,12 @@
     pl.semaphore_wait(barrier, len(peers))
     own_n.start()
 
-    def start_z(k, carry):
+    def start_z(k):
         for d in range(3):
             z_copy(k, d).start()
-        return carry
-
-    lax.fori_loop(0, HALF, start_z, 0)
+
+    start_z(0)
+    start_z(1)
 
     wqt[...] = wq_ref[...].astype(jnp.float32).T.astype(jnp.bfloat16)
     wvt[...] = wv_ref[...].astype(jnp.float32).T.astype(jnp.bfloat16)
@@ -167,12 +172,20 @@
         tile[h] = raw[pl.ds(h, BLOCK, stride=HEADS), :].T.astype(jnp.bfloat16)
     own_b.start()
 
-    def start_b(h, carry):
+    def start_b(h):
         for d in range(3):
             b_copy(h, d).start()
-        return carry
-
-    lax.fori_loop(0, HEADS, start_b, 0)
+
+    start_b(0)
+    start_b(1)
+    start_b(2)
+    start_z(2)
+    start_b(3)
+    start_b(4)
+    start_z(3)
+    start_b(5)
+    start_b(6)
+    start_b(7)
     own_b.wait()
 
     def project(r):
@@ -197,28 +210,49 @@
 
         lax.fori_loop(0, 4, part, 0)
 
-    def attend(r, h):
+    def scores(r, h):
         qt = q_scr[r]
         channel = lax.broadcasted_iota(jnp.int32, qt.shape, 0)
         qm = jnp.where((channel >= h * size) & (channel < (h + 1) * size), qt, jnp.zeros_like(qt))
-        top = None
-        for at in range(0, keys, STEP):
-            scores = jnp.dot(k_scr[r, pl.ds(at, STEP), :], qm, preferred_element_type=jnp.float32)
-            parts = []
+
+        def block(at, s_ref, top):
+            part = jnp.dot(k_scr[r, pl.ds(at, STEP), :], qm, preferred_element_type=jnp.float32)
+            biases = []
             for sub in range(at // BLOCK, (at + STEP) // BLOCK):
                 j = (sub % 4) * 4 + sub // 4
                 here = (h, j % 2, (j // 2) % 4, j // 8)
-                parts.append(jnp.concatenate([ball[here + (0,)], ball[here + (1,)]], axis=1))
-            scores = scores + jnp.concatenate(parts, axis=0).astype(jnp.float32)
-            s_scr[pl.ds(at, STEP), :] = scores
-            best = jnp.max(scores, axis=0, keepdims=True)
-            top = best if top is None else jnp.maximum(top, best)
-        acc = None
+                biases.append(jnp.concatenate([ball[here + (0,)], ball[here + (1,)]], axis=1))
+            part = part + jnp.concatenate(biases, axis=0).astype(jnp.float32)
+            s_ref[pl.ds(at, STEP), :] = part
+            best = jnp.max(part.reshape(STEP // 8, 8, part.shape[1]), axis=0)
+            return best if top is None else jnp.maximum(top, best)
+
+        return block
+
+    def mix(r, h, t_ref):
+        top = jnp.max(t_ref[...], axis=0, keepdims=True)
+
+        def block(at, s_ref, acc):
+            weights = jnp.exp(s_ref[pl.ds(at, STEP), :] - top).astype(jnp.bfloat16)
+            part = jnp.dot(v_scr[r, h, :, pl.ds(at, STEP)], weights, preferred_element_type=jnp.float32)
+            return part if acc is None else acc + part
+
+        return block
+
+    def attend(new, s_new, t_new, old, s_old, t_old):
+        top = acc = None
+        score = None if new is None else scores(*new)
+        mixed = None if old is None else mix(*old, t_old)
         for at in range(0, keys, STEP):
-            weights = jnp.exp(s_scr[pl.ds(at, STEP), :] - top).astype(jnp.bfloat16)
-            part = jnp.dot(v_scr[r, h, :, pl.ds(at, STEP)], weights, preferred_element_type=jnp.float32)
-            acc = part if acc is None else acc + part
-        a_scr[r, pl.ds(pl.multiple_of(h * size, size), size), :] = acc[:size] / acc[size:size + 1]
+            if score is not None:
+                top = score(at, s_new, top)
+            if mixed is not None:
+                acc = mixed(at, s_old, acc)
+        if score is not None:
+            t_new[...] = top
+        if mixed is not None:
+            r, h = old
+            a_scr[r, pl.ds(pl.multiple_of(h * size, size), size), :] = acc[:size] / acc[size:size + 1]
 
     def finish(r):
         gated = (g_scr[r] * a_scr[r].T).astype(jnp.bfloat16)
@@ -227,71 +261,65 @@
         out_copy(r).start()
         out_ref[qh * HALF + r] = upd[r, pl.ds(pl.multiple_of(qh * BLOCK, BLOCK), BLOCK), :]
 
-    tile_rows, tile_heads = [t[0] for t in TILES], [t[1] for t in TILES]
-
-    def run_tile(i, carry):
-        r, h = lookup(tile_rows, i), lookup(tile_heads, i)
-        attend(r, h)
-        pl.when(h == HEADS - 1)(lambda: finish(r))
-        return carry
-
-    def run_tiles(first, last):
-        lax.fori_loop(first, last, run_tile, 0)
-
-    def tick(t, done):
-        even = t % 2 == 0
-        k = t // 2
-        after = [lookup([d[p] for d in DONE], t) for p in range(3)]
-
-        @pl.when(t < HEADS)
-        def _():
-            for d in range(3):
-                b_copy(t, d).wait_recv()
-            for d in range(2):
-                y_copy(t, d).start()
-
-        @pl.when(even & (k < HALF))
-        def _():
-            for d in range(2):
-                x_copy(k, d).wait_recv()
-            for d in range(2):
-                x_forward(k, d).start()
-
-        @pl.when(t >= 2)
-        def _():
-            c_copy(t - 2).wait_recv()
-
-        run_tiles(done, after[0])
-
-        @pl.when((t >= 1) & (t <= HEADS))
-        def _():
-            for d in range(2):
-                y_forward(t - 1, d).wait_recv()
-            c_copy(t - 1).start()
-
-        @pl.when(even & (k < HALF - 1))
-        def _():
-            wait_z(k + 1)
-
-        run_tiles(after[0], after[1])
-
-        @pl.when(t < HEADS)
-        def _():
-            for d in range(2):
-                y_copy(t, d).wait_recv()
-            for d in range(2):
-                y_forward(t, d).start()
-
-        @pl.when(even & (k < HALF))
-        def _():
-            for d in range(2):
-                x_forward(k, d).wait_recv()
-            project(k)
-
-        run_tiles(after[1], after[2])
-        return after[2]
-
-    lax.fori_loop(0, len(DONE), tick, jnp.int32(0))
+    def row_z(k):
+        wait_z(k)
+
+    def row_x(k):
+        for d in range(2):
+            x_copy(k, d).wait_recv()
+        for d in range(2):
+            x_forward(k, d).start()
+
+    def row_last(k):
+        for d in range(2):
+            x_forward(k, d).wait_recv()
+        project(k)
+
+    def head_z(h):
+        for d in range(3):
+            b_copy(h, d).wait_recv()
+        for d in range(2):
+            y_copy(h, d).start()
+
+    def head_y(h):
+        for d in range(2):
+            y_copy(h, d).wait_recv()
+        for d in range(2):
+            y_forward(h, d).start()
+
+    def head_last(h):
+        for d in range(2):
+            y_forward(h, d).wait_recv()
+        c_copy(h).start()
+
+    def head_core(h):
+        c_copy(h).wait_recv()
+
+    def tile_at(i):
+        at = unpacked(TILES, 5, i)
+        return at // HEADS, at % HEADS
+
+    even, odd = (s_even, t_even), (s_odd, t_odd)
+
+    def run_tile(i):
+        new, old = tile_at(i), tile_at(jnp.maximum(i - 1, 0))
+        pl.when(i == 0)(lambda: attend(new, *even, None, *odd))
+        pl.when(i % 2 == 1)(lambda: attend(new, *odd, old, *even))
+        pl.when((i > 0) & (i % 2 == 0))(lambda: attend(new, *even, old, *odd))
+        pl.when((i > 0) & (old[1] == HEADS - 1))(lambda: finish(old[0]))
+
+    actions = (row_z, row_x, row_last, head_z, head_y, head_last, head_core, run_tile)
+
+    def step(n, counts):
+        kind = unpacked(STEPS, 3, n)
+        for at, action in enumerate(actions):
+            pl.when(kind == at)(lambda action=action, at=at: action(counts[at]))
+        return tuple(count + (kind == at).astype(jnp.int32) for at, count in enumerate(counts))
+
+    lax.fori_loop(0, len(STEPS), step, (jnp.int32(1),) + (jnp.int32(0),) * 7)
+    last = (TILES[-1] // HEADS, TILES[-1] % HEADS)
+    attend(None, *even, last, *odd)
+    finish(last[0])
 
     def close_rows(k, carry):
         out_copy(k).wait_recv()
@@ -355,6 +383,9 @@
             pltpu.VMEM((HALF, 2 * block, depth), f32),
             pltpu.VMEM((HALF, depth, 2 * block), f32),
             pltpu.VMEM((keys, 2 * block), f32),
+            pltpu.VMEM((keys, 2 * block), f32),
+            pltpu.VMEM((8, 2 * block), f32),
+            pltpu.VMEM((8, 2 * block), f32),
             pltpu.VMEM((HALF, 2 * block, depth), bf),
             pltpu.VMEM((depth, depth), bf),
             pltpu.VMEM((depth, depth), bf),

time: 131 us -> 99.8 us (0.76); the launches traced: 129 us -> 99.5 us
  Pallas kernels: 127 us -> 97.6 us
    pallas_call x1, Pallas kernels: 127 us -> 97.6 us  [body(): pl.pallas_call(fused_kernel, out_shape=jax.ShapeDtypeStruct((rows, block,...]
where the time goes in v3:
time: 99.8 us; the launch traced here: 99.5 us
  Pallas kernels  97.6 us (98%)
  local copies, waits for them, and re-layouts  1.87 us (2%)
    pallas_call x1, Pallas kernels, body(): pl.pallas_call(fused_kernel, out_shape=jax.ShapeDtypeStruct((rows, block,...  97.6 us

profile of v3, /device:TPU:6, one launch (start us, length us, event | category | flops | bytes accessed | tf_op | source)
XLA Modules:
  0.0 99.5 jit_solution(14163738431616358279)
XLA Ops:
  0.0 97.6 %shard_map.100 = bf16[8,128,256]{2,1,0:T(8,128)(2,1)} custom-call(bf16[8,128,256]{2,1,0:T(8,128)(2,1)} %m_ref.1, bf16[128,128,128]{2,1,0:T(8,128)(2,1)} %pair_ref.1, bf16[256,256]{1,0:T(8,128)(2,1)} %wq_ref.1, bf16[256,256]{1,0:T(8,128)(2,1)} %wk_ref.1, bf16[256,256]{1,0:T(8,128)(2,1)} %wv_ref.1, bf16[256,256]{1,0:T(8,128)(2,1)} %wf_ref.1, ...), custom_call_target="tpu_custom_call" | custom-call | tf_op jit(solution)/shard_map/pallas_call | solution.py:368
  97.7 1.9 %copy.12 = bf16[8,128,256]{2,1,0:T(8,128)(2,1)} copy(bf16[8,128,256]{2,1,0:T(8,128)(2,1)} %shard_map.100) | data formatting | bytes 1048576

commit v4 on v3

v4 whole, which is shorter than its diff:
```python
import jax
import jax.numpy as jnp
from jax import lax
from jax.experimental import pallas as pl
from jax.experimental.pallas import tpu as pltpu
from jax.sharding import PartitionSpec as P

MESH = pl.DeviceIdType.MESH
VMEM_LIMIT = 62 * 1024 * 1024
NT = (((1,), (1,)), ((), ()))
HEADS = 8
HALF = 4
BLOCK = 128
STEP = 256
FORWARDED = (2, 6)
STEPS = (
    0, 6, 2, 2, 1, 6, 3, 4, 6, 0, 6, 6, 5, 7, 2, 3, 4, 2, 5, 7, 3, 0, 6, 3, 1,
    6, 6, 4, 6, 7, 2, 7, 5, 7, 4, 7, 2, 5, 7, 7, 3, 0, 6, 3, 1, 6, 6, 6, 7, 4,
    2, 7, 7, 7, 4, 5, 2, 7, 7, 7, 5, 7, 7, 7, 3, 4, 1, 6, 6, 6, 7, 5, 7, 7, 3,
    4, 7, 7, 7, 5, 7, 7, 7, 7, 7, 7, 7, 7,
)
TILES = (
    0, 1, 8, 9, 2, 10, 3, 11, 16, 17, 18, 19, 4, 12, 20, 5,
    13, 21, 24, 25, 26, 27, 28, 29, 6, 14, 22, 30, 7, 15, 23, 31,
)
PARTS = (
    0, 1, 2, 3, 4, 8, 5, 6, 7, 12, 9, 10, 11, 13, 14, 15,
)


def forwarded(h):
    return (h >= FORWARDED[0]) & (h < FORWARDED[1])


def packed(values, bits):
    per = 30 // bits
    return per, [sum(v << (bits * at) for at, v in enumerate(values[i:i + per])) for i in range(0, len(values), per)]


def unpacked(values, bits, index):
    per, words = packed(values, bits)
    word = lookup(words, index // per)
    return (word >> (bits * (index % per))) % (1 << bits)


def lookup(table, index):
    value = jnp.int32(table[0])
    for at in range(1, len(table)):
        value = jnp.where(index >= at, jnp.int32(table[at]), value)
    return value


def standardize_features(x):
    x = x.astype(jnp.float32)
    mean = jnp.mean(x, axis=-1, keepdims=True)
    var = jnp.mean((x - mean) ** 2, axis=-1, keepdims=True)
    return (x - mean) * lax.rsqrt(var + 1e-05)


def fused_kernel(
    m_ref, pair_ref, wq_ref, wk_ref, wv_ref, wf_ref, off_ref, wc_ref, wo_ref, oo_ref,
    out_ref,
    nown, nall, tile, ball, pair_buf, raw, k_scr, v_scr, q_scr, g_scr, g_own, g_send, s_even, s_odd, t_even, t_odd, wqt, wvt, wft, wot, offsets,
    psem, lsem, zs, zr, xs, xr, bs, br, ys, yr, cs, cr, os, orr,
):
    s, res = lax.axis_index("seq"), lax.axis_index("res")
    c, y, zh, x, zl = s % 2, (s // 2) % 4, s // 8, res % 4, res // 4
    qh = zl // 2
    depth = wq_ref.shape[0]
    size = depth // HEADS
    keys = k_scr.shape[1]
    scale = 1.0 / size**0.5

    def device(c_=c, y_=y, zh_=zh, x_=x, zl_=zl):
        return (zh_ * 8 + y_ * 2 + c_, zl_ * 4 + x_)

    z_peers = [device(zl_=(zl + d) % 4) for d in (1, 2, 3)]
    x_peers = [device(x_=(x + d) % 4) for d in (1, 2, 3)]
    y_peers = [device(y_=(y + d) % 4) for d in (1, 2, 3)]
    partner = device(zl_=(zl + 2) % 4)
    b_peers = [partner, device(zh_=1 - zh), device(zh_=1 - zh, zl_=(zl + 2) % 4)]
    sibling = device(c_=1 - c)
    peers = z_peers + x_peers + y_peers + b_peers[1:] + [sibling]

    barrier = pltpu.get_barrier_semaphore()
    for peer in peers:
        pl.semaphore_signal(barrier, inc=1, device_id=peer, device_id_type=MESH)

    chunk = BLOCK // 4

    def pair_copy(i):
        at = pl.ds(i * chunk, chunk)
        return pltpu.make_async_copy(pair_ref.at[at], pair_buf.at[at], psem.at[i])

    for i in range(4):
        pair_copy(i).start()

    def norm_rows(k, carry):
        for i in (k, HALF + k):
            nown[i] = standardize_features(m_ref[i]).astype(jnp.bfloat16)
        return carry

    norm_rows(0, 0)

    def remote(src, dst, send, recv, peer):
        return pltpu.make_async_remote_copy(
            src_ref=src, dst_ref=dst, send_sem=send, recv_sem=recv, device_id=peer, device_id_type=MESH
        )

    def z_copy(k, d):
        to = (zl + d + 1) % 4
        return remote(nown.at[(to // 2) * HALF + k], nall.at[k, x, zl], zs.at[k, d], zr.at[k, d], z_peers[d])

    def x_copy(k, d):
        return remote(nall.at[k, x], nall.at[k, x], xs.at[k, d], xr.at[k, d], x_peers[d])

    def b_copy(h, d):
        return remote(tile.at[h], ball.at[h, c, y, zh, qh], bs.at[h, d], br.at[h, d], b_peers[d])

    def y_copy(h, d):
        return remote(ball.at[h, c, y], ball.at[h, c, y], ys.at[h, d], yr.at[h, d], y_peers[d])

    def y_forward(h, d):
        block = ball.at[h, c, (y + 3) % 4, 0] if d == 0 else ball.at[h, c, (y + 1) % 4, 1]
        return remote(block, block, ys.at[h, 1 + 2 * d], yr.at[h, 1 + 2 * d], y_peers[2 * d])

    def c_copy(h):
        return remote(ball.at[h, c], ball.at[h, c], cs.at[h], cr.at[h], sibling)

    def g_copy(r, h):
        at = pl.ds(pl.multiple_of(h * size, size), size)
        return remote(g_send.at[r, at], g_own.at[qh * HALF + r, at], os.at[r, h], orr.at[r, h], partner)

    own_n = pltpu.make_async_copy(nown.at[pl.ds(qh * HALF, HALF)], nall.at[:, x, zl], lsem.at[0])
    own_b = pltpu.make_async_copy(tile, ball.at[:, c, y, zh, qh], lsem.at[1])

    pl.semaphore_wait(barrier, len(peers))

    def start_z(k):
        for d in range(3):
            z_copy(k, d).start()

    start_z(0)

    wc = wc_ref[...]
    group = 16

    def pair_rows(i, carry):
        at = pl.multiple_of(i * group, group)
        normed = standardize_features(pair_buf[pl.ds(at, group)]).astype(jnp.bfloat16)
        for j in range(group):
            raw[pl.ds(pl.multiple_of((at + j) * HEADS, HEADS), HEADS), :] = lax.dot_general(
                wc, normed[j], NT, preferred_element_type=jnp.float32
            )
        return carry

    def gates(r):
        first = zl % 2
        rows_q = jnp.concatenate([nall[r, x, first], nall[r, x, first + 2]], axis=0)
        q = lax.dot_general(wqt[...], rows_q, NT, preferred_element_type=jnp.float32) * scale
        q_scr[r] = q.astype(jnp.bfloat16)
        gate = lax.dot_general(wft[...], rows_q, NT, preferred_element_type=jnp.float32)
        offset = jnp.concatenate([offsets[...], offsets[...]], axis=1)
        g_scr[r] = jax.nn.sigmoid(gate + offset)

    def project(r, i):
        rows = nall[r, i].reshape(4 * BLOCK, depth)
        at = pl.multiple_of(i * 4 * BLOCK, 4 * BLOCK)
        k_scr[r, pl.ds(at, 4 * BLOCK), :] = jnp.dot(
            rows, wk_ref[...], preferred_element_type=jnp.float32
        ).astype(jnp.bfloat16)
        v = lax.dot_general(wvt[...], rows, NT, preferred_element_type=jnp.float32).astype(jnp.bfloat16)
        for h in range(HEADS):
            v_scr[r, h, pl.ds(0, size), pl.ds(at, 4 * BLOCK)] = v[h * size:(h + 1) * size]

    def row_z(k):
        for d in range(3):
            z_copy(k, d).wait_recv()
        for d in range(3):
            x_copy(k, d).start()

    for i in range(4):
        pair_copy(i).wait()
        lax.fori_loop(i * (chunk // group), (i + 1) * (chunk // group), pair_rows, 0)
    for h in range(HEADS):
        tile[h] = raw[pl.ds(h, BLOCK, stride=HEADS), :].T.astype(jnp.bfloat16)
    own_b.start()

    def start_b(h):
        for d in range(3):
            b_copy(h, d).start()

    start_b(0)
    start_b(1)
    lax.fori_loop(1, HALF, norm_rows, 0)
    own_n.start()
    start_z(1)
    start_b(2)
    start_b(3)
    start_z(2)
    start_b(4)
    start_b(5)
    start_z(3)
    start_b(6)
    start_b(7)
    wqt[...] = wq_ref[...].astype(jnp.float32).T.astype(jnp.bfloat16)
    wvt[...] = wv_ref[...].astype(jnp.float32).T.astype(jnp.bfloat16)
    wft[...] = wf_ref[...].astype(jnp.float32).T.astype(jnp.bfloat16)
    wot[...] = wo_ref[...].astype(jnp.float32).T.astype(jnp.bfloat16)
    offsets[...] = jnp.broadcast_to(off_ref[...], (BLOCK, depth)).T
    for r in range(HALF):
        v_scr[r, :, pl.ds(size, 16), :] = jnp.ones((HEADS, 16, keys), jnp.bfloat16)

    own_n.wait()
    own_b.wait()

    def scores(r, h):
        qt = q_scr[r]
        channel = lax.broadcasted_iota(jnp.int32, qt.shape, 0)
        qm = jnp.where((channel >= h * size) & (channel < (h + 1) * size), qt, jnp.zeros_like(qt))

        def block(at, s_ref, top):
            part = jnp.dot(k_scr[r, pl.ds(at, STEP), :], qm, preferred_element_type=jnp.float32)
            biases = []
            for sub in range(at // BLOCK, (at + STEP) // BLOCK):
                j = (sub % 4) * 4 + sub // 4
                here = (h, j % 2, (j // 2) % 4, j // 8)
                biases.append(jnp.concatenate([ball[here + (0,)], ball[here + (1,)]], axis=1))
            part = part + jnp.concatenate(biases, axis=0).astype(jnp.float32)
            s_ref[pl.ds(at, STEP), :] = part
            best = jnp.max(part.reshape(STEP // 8, 8, part.shape[1]), axis=0)
            return best if top is None else jnp.maximum(top, best)

        return block

    def mix(r, h, t_ref):
        top = jnp.max(t_ref[...], axis=0, keepdims=True)

        def block(at, s_ref, acc):
            weights = jnp.exp(s_ref[pl.ds(at, STEP), :] - top).astype(jnp.bfloat16)
            part = jnp.dot(v_scr[r, h, :, pl.ds(at, STEP)], weights, preferred_element_type=jnp.float32)
            return part if acc is None else acc + part

        return block

    def attend(new, s_new, t_new, old, s_old, t_old):
        top = acc = None
        score = None if new is None else scores(*new)
        mixed = None if old is None else mix(*old, t_old)
        for at in range(0, keys, STEP):
            if score is not None:
                top = score(at, s_new, top)
            if mixed is not None:
                acc = mixed(at, s_old, acc)
        if score is not None:
            t_new[...] = top
        if mixed is not None:
            r, h = old
            at = pl.ds(pl.multiple_of(h * size, size), size)
            gated = (g_scr[r, at, :] * (acc[:size] / acc[size:size + 1])).astype(jnp.bfloat16)
            left, right = gated[:, :BLOCK], gated[:, BLOCK:]
            g_own[qh * HALF + r, at, :] = jnp.where(qh == 0, left, right)
            g_send[r, at, :] = jnp.where(qh == 0, right, left)
            g_copy(r, h).start()

    def finish(r, carry):
        update = jnp.dot(wot[...], g_own[r], preferred_element_type=jnp.float32).T + oo_ref[...]
        out_ref[r] = update.astype(jnp.bfloat16)
        return carry

    def row_x(k):
        for d in range(3):
            x_copy(k, d).wait_recv()

    def head_z(h):
        for d in range(3):
            b_copy(h, d).wait_recv()
        y_copy(h, 0).start()
        y_copy(h, 2).start()
        pl.when(jnp.logical_not(forwarded(h)))(lambda: y_copy(h, 1).start())

    def head_y(h):
        y_copy(h, 0).wait_recv()
        y_copy(h, 2).wait_recv()

        @pl.when(forwarded(h))
        def _():
            for d in range(2):
                y_forward(h, d).start()

        @pl.when(jnp.logical_not(forwarded(h)))
        def _():
            y_copy(h, 1).wait_recv()
            c_copy(h).start()

    def head_last(h):
        @pl.when(forwarded(h))
        def _():
            for d in range(2):
                y_forward(h, d).wait_recv()
            c_copy(h).start()

    def head_core(h):
        c_copy(h).wait_recv()

    def tile_at(i):
        at = unpacked(TILES, 5, i)
        return at // HEADS, at % HEADS

    def run_part(i):
        at = unpacked(PARTS, 4, i)
        r, d = at // 4, at % 4
        pl.when(d == 0)(lambda: gates(r))
        project(r, (x + d) % 4)

    even, odd = (s_even, t_even), (s_odd, t_odd)

    def run_tile(i):
        new, old = tile_at(i), tile_at(jnp.maximum(i - 1, 0))
        pl.when(i == 0)(lambda: attend(new, *even, None, *odd))
        pl.when(i % 2 == 1)(lambda: attend(new, *odd, old, *even))
        pl.when((i > 0) & (i % 2 == 0))(lambda: attend(new, *even, old, *odd))

    actions = (row_z, row_x, head_z, head_y, head_last, head_core, run_part, run_tile)

    def step(n, counts):
        kind = unpacked(STEPS, 3, n)
        for at, action in enumerate(actions):
            pl.when(kind == at)(lambda action=action, at=at: action(counts[at]))
        return tuple(count + (kind == at).astype(jnp.int32) for at, count in enumerate(counts))

    lax.fori_loop(0, len(STEPS), step, (jnp.int32(0),) * 8)
    last = (TILES[-1] // HEADS, TILES[-1] % HEADS)
    attend(None, *even, last, *odd)
    own_rows = qh * HALF
    lax.fori_loop(own_rows, own_rows + HALF, finish, 0)

    def close_tiles(i, carry):
        g_copy(i // HEADS, i % HEADS).wait_recv()
        return carry

    lax.fori_loop(0, HALF * HEADS, close_tiles, 0)
    lax.fori_loop(HALF - own_rows, 2 * HALF - own_rows, finish, 0)

    def close_rows(k, carry):
        for d in range(3):
            z_copy(k, d).wait_send()
        for d in range(3):
            x_copy(k, d).wait_send()
        for h in range(HEADS):
            g_copy(k, h).wait_send()
        return carry

    def close_heads(h, carry):
        for d in range(3):
            b_copy(h, d).wait_send()
        y_copy(h, 0).wait_send()
        y_copy(h, 2).wait_send()
        pl.when(jnp.logical_not(forwarded(h)))(lambda: y_copy(h, 1).wait_send())

        @pl.when(forwarded(h))
        def _():
            for d in range(2):
                y_forward(h, d).wait_send()

        c_copy(h).wait_send()
        return carry

    lax.fori_loop(0, HEADS, close_heads, 0)
    lax.fori_loop(0, HALF, close_rows, 0)


def body(
    alignment_embedding,
    coupling_embedding,
    asking_projection,
    lookup_projection,
    content_projection,
    filter_projection,
    filter_offset,
    coupling_head_projection,
    final_projection,
    final_offset,
):
    rows, block, depth = alignment_embedding.shape
    heads = coupling_head_projection.shape[1]
    size = depth // heads
    keys = 16 * block
    bf, f32 = jnp.bfloat16, jnp.float32
    sem = pltpu.SemaphoreType.DMA
    vmem = pl.BlockSpec(memory_space=pltpu.VMEM)
    in_specs = [vmem] * 10
    in_specs[1] = pl.BlockSpec(memory_space=pl.ANY)
    return pl.pallas_call(
        fused_kernel,
        out_shape=jax.ShapeDtypeStruct((rows, block, depth), bf),
        in_specs=in_specs,
        out_specs=vmem,
        scratch_shapes=[
            pltpu.VMEM((rows, block, depth), bf),
            pltpu.VMEM((HALF, 4, 4, block, depth), bf),
            pltpu.VMEM((heads, block, block), bf),
            pltpu.VMEM((heads, 2, 4, 2, 2, block, block), bf),
            pltpu.VMEM((block, block, coupling_embedding.shape[2]), bf),
            pltpu.VMEM((block * heads, block), f32),
            pltpu.VMEM((HALF, keys, depth), bf),
            pltpu.VMEM((HALF, heads, size + 16, keys), bf),
            pltpu.VMEM((HALF, depth, 2 * block), bf),
            pltpu.VMEM((HALF, depth, 2 * block), f32),
            pltpu.VMEM((rows, depth, block), bf),
            pltpu.VMEM((HALF, depth, block), bf),
            pltpu.VMEM((keys, 2 * block), f32),
            pltpu.VMEM((keys, 2 * block), f32),
            pltpu.VMEM((8, 2 * block), f32),
            pltpu.VMEM((8, 2 * block), f32),
            pltpu.VMEM((depth, depth), bf),
            pltpu.VMEM((depth, depth), bf),
            pltpu.VMEM((depth, depth), bf),
            pltpu.VMEM((depth, depth), bf),
            pltpu.VMEM((depth, block), f32),
            sem((4,)),
            sem((2,)),
            sem((HALF, 3)),
            sem((HALF, 3)),
            sem((HALF, 4)),
            sem((HALF, 4)),
            sem((heads, 3)),
            sem((heads, 3)),
            sem((heads, 4)),
            sem((heads, 4)),
            sem((heads,)),
            sem((heads,)),
            sem((HALF, heads)),
            sem((HALF, heads)),
        ],
        compiler_params=pltpu.CompilerParams(
            collective_id=0, has_side_effects=True, vmem_limit_bytes=VMEM_LIMIT
        ),
    )(
        alignment_embedding, coupling_embedding, asking_projection, lookup_projection, content_projection,
        filter_projection, filter_offset.reshape(1, depth), coupling_head_projection.T, final_projection,
        final_offset.reshape(1, depth),
    )


def solution(mesh):
    placed = (P("seq", "res", None), P("res", "seq", None), P(), P(), P(), P(), P(), P(), P(), P())
    return jax.shard_map(
        body, mesh=mesh, in_specs=placed, out_specs=P("seq", "res", None), check_vma=False
    )
```

time: 99.8 us -> 96.2 us (0.964)
  Pallas kernels: 97.6 us -> 94.2 us
    pallas_call x1, Pallas kernels: 97.6 us -> 94.2 us  [body(): pl.pallas_call(fused_kernel, out_shape=jax.ShapeDtypeStruct((rows, block,...]
where the time goes in v4:
time: 96.2 us; the launch traced here: 96 us
  Pallas kernels  94.2 us (98%)
  local copies, waits for them, and re-layouts  1.87 us (2%)
    pallas_call x1, Pallas kernels, body(): pl.pallas_call(fused_kernel, out_shape=jax.ShapeDtypeStruct((rows, block,...  94.2 us

profile of v4, /device:TPU:6, one launch (start us, length us, event | category | flops | bytes accessed | tf_op | source)
XLA Modules:
  0.0 96.0 jit_solution(4503487543497058310)
XLA Ops:
  0.0 94.2 %shard_map.100 = bf16[8,128,256]{2,1,0:T(8,128)(2,1)} custom-call(bf16[8,128,256]{2,1,0:T(8,128)(2,1)} %m_ref.1, bf16[128,128,128]{2,1,0:T(8,128)(2,1)} %pair_ref.1, bf16[256,256]{1,0:T(8,128)(2,1)} %wq_ref.1, bf16[256,256]{1,0:T(8,128)(2,1)} %wk_ref.1, bf16[256,256]{1,0:T(8,128)(2,1)} %wv_ref.1, bf16[256,256]{1,0:T(8,128)(2,1)} %wf_ref.1, ...), custom_call_target="tpu_custom_call" | custom-call | tf_op jit(solution)/shard_map/pallas_call | solution.py:394
  94.2 1.9 %copy.12 = bf16[8,128,256]{2,1,0:T(8,128)(2,1)} copy(bf16[8,128,256]{2,1,0:T(8,128)(2,1)} %shard_map.100) | data formatting | bytes 1048576

commit v5 on v4

--- a/solution.py
+++ b/solution.py
@@ -208,8 +208,6 @@
     wft[...] = wf_ref[...].astype(jnp.float32).T.astype(jnp.bfloat16)
     wot[...] = wo_ref[...].astype(jnp.float32).T.astype(jnp.bfloat16)
     offsets[...] = jnp.broadcast_to(off_ref[...], (BLOCK, depth)).T
-    for r in range(HALF):
-        v_scr[r, :, pl.ds(size, 16), :] = jnp.ones((HEADS, 16, keys), jnp.bfloat16)
 
     own_n.wait()
     own_b.wait()
@@ -237,9 +235,12 @@
         top = jnp.max(t_ref[...], axis=0, keepdims=True)
 
         def block(at, s_ref, acc):
-            weights = jnp.exp(s_ref[pl.ds(at, STEP), :] - top).astype(jnp.bfloat16)
-            part = jnp.dot(v_scr[r, h, :, pl.ds(at, STEP)], weights, preferred_element_type=jnp.float32)
-            return part if acc is None else acc + part
+            weights = jnp.exp(s_ref[pl.ds(at, STEP), :] - top)
+            total = jnp.sum(weights.reshape(STEP // 8, 8, weights.shape[1]), axis=0)
+            part = jnp.dot(
+                v_scr[r, h, :, pl.ds(at, STEP)], weights.astype(jnp.bfloat16), preferred_element_type=jnp.float32
+            )
+            return (part, total) if acc is None else (acc[0] + part, acc[1] + total)
 
         return block
 
@@ -257,7 +258,7 @@
         if mixed is not None:
             r, h = old
             at = pl.ds(pl.multiple_of(h * size, size), size)
-            gated = (g_scr[r, at, :] * (acc[:size] / acc[size:size + 1])).astype(jnp.bfloat16)
+            gated = (g_scr[r, at, :] * (acc[0] / jnp.sum(acc[1], axis=0, keepdims=True))).astype(jnp.bfloat16)
             left, right = gated[:, :BLOCK], gated[:, BLOCK:]
             g_own[qh * HALF + r, at, :] = jnp.where(qh == 0, left, right)
             g_send[r, at, :] = jnp.where(qh == 0, right, left)
@@ -404,7 +405,7 @@
             pltpu.VMEM((block, block, coupling_embedding.shape[2]), bf),
             pltpu.VMEM((block * heads, block), f32),
             pltpu.VMEM((HALF, keys, depth), bf),
-            pltpu.VMEM((HALF, heads, size + 16, keys), bf),
+            pltpu.VMEM((HALF, heads, size, keys), bf),
             pltpu.VMEM((HALF, depth, 2 * block), bf),
             pltpu.VMEM((HALF, depth, 2 * block), f32),
             pltpu.VMEM((rows, depth, block), bf),

time: 96.2 us -> 95.9 us (level)
  no operation moved by 1% of the time
where the time goes in v5:
time: 95.9 us; the launch traced here: 95.8 us
  Pallas kernels  93.9 us (98%)
  local copies, waits for them, and re-layouts  1.87 us (2%)
    pallas_call x1, Pallas kernels, body(): pl.pallas_call(fused_kernel, out_shape=jax.ShapeDtypeStruct((rows, block,...  93.9 us

profile of v5, /device:TPU:6, one launch (start us, length us, event | category | flops | bytes accessed | tf_op | source)
XLA Modules:
  0.0 95.8 jit_solution(11254273138008564182)
XLA Ops:
  0.0 93.9 %shard_map.100 = bf16[8,128,256]{2,1,0:T(8,128)(2,1)} custom-call(bf16[8,128,256]{2,1,0:T(8,128)(2,1)} %m_ref.1, bf16[128,128,128]{2,1,0:T(8,128)(2,1)} %pair_ref.1, bf16[256,256]{1,0:T(8,128)(2,1)} %wq_ref.1, bf16[256,256]{1,0:T(8,128)(2,1)} %wk_ref.1, bf16[256,256]{1,0:T(8,128)(2,1)} %wv_ref.1, bf16[256,256]{1,0:T(8,128)(2,1)} %wf_ref.1, ...), custom_call_target="tpu_custom_call" | custom-call | tf_op jit(solution)/shard_map/pallas_call | solution.py:395
  93.9 1.9 %copy.12 = bf16[8,128,256]{2,1,0:T(8,128)(2,1)} copy(bf16[8,128,256]{2,1,0:T(8,128)(2,1)} %shard_map.100) | data formatting | bytes 1048576
